TPU v7x, 32 devices: a whole 2x2x4 slice. The times are simulated.
32 devices in a mesh: gx: 8 (over z, core), gy: 4 (over y, x).
Axes of the slice: x: 2, y: 2, z: 4, core: 2. Of those that a mesh axis runs over, the one named last changes fastest.
Arguments:
- solution: float32 [512, 4096], P(None, ('gx', 'gy')), may hold values from -6 to 6
- residual: float32 [512, 4096], P(None, ('gx', 'gy')), may hold values from -60 to 60
- metric_diag: bfloat16 [3, 512, 4096], P(None, None, ('gx', 'gy')), may hold values from 0.039794922 to 0.3984375
- metric_cross: bfloat16 [3, 512, 4096], P(None, None, ('gx', 'gy')), may hold values from -0.017944336 to 0.017944336
- fdm_vectors: float32 [3, 8, 8, 4096], P(None, None, None, ('gx', 'gy')), may hold values from -5 to 5
- fdm_values: float32 [3, 8, 4096], P(None, None, ('gx', 'gy')), may hold values from 0.05 to 20
- vertex_ids: int32 [8, 4096], P(None, ('gx', 'gy')), may hold values from 0 to 511
- coarse_inverse: float32 [512, 512], P(('gx', 'gy')), may hold values from -0.2 to 0.2, as said below
- elem_live: int32 [32], P(('gx', 'gy')), may hold values from 80 to 128, as said below
- section_face: int32 [32, 4, 20], P(('gx', 'gy')), may hold values from -1 to 767, as said below
- section_code: int32 [32, 4, 20], P(('gx', 'gy')), may hold values from 0 to 7, as said below
- pipe_face: int32 [32, 2, 64], P(('gx', 'gy')), may hold values from 0 to 767, as said below
- pipe_code: int32 [32, 2, 64], P(('gx', 'gy')), may hold values from 0 to 7, as said below
Outputs:
- solution_out: float32 [512, 4096], P(None, ('gx', 'gy'))
- residual_out: float32 [512, 4096], P(None, ('gx', 'gy'))
- norm_ratio: float32 [1], replicated
Inputs may be any that keep to these rules, and one draw needn't show every extreme that they name: `elem_live`: one device holds all 128 slots in every draw. A face id 6 e + f names face f of slot e of the device, with e below the device's elem_live; no id appears twice on a device over section_face and pipe_face; -1 marks an empty slot, and in each peer's row the slots holding faces come first. Slot (q, c) of device (x, y) holds a face exactly when slot (y, c) of device (x, q) does; in the row q = y they come in pairs (c, c xor 1). Each device's rows for peers y - 1, y + 1 and y + 4 / 2 (mod 4) are full; rows for other peers more than two places away (mod 4) are empty. `section_code`: with inv(o) = o for o < 4 and 4 + 2 (o mod 2) + floor((o mod 4) / 2) for o >= 4, the codes of two paired slots are inv of each other; empty slots hold 0. `pipe_face`: every slot holds a face, as for section_face. `pipe_code`: the codes of two paired slots are inv of each other, as for section_code. `coarse_inverse`: Symmetric.
All inputs are finite; a program needn't handle non-finite values.
Results may differ from a plain program's by a relative error of at most 0.0003.
Values sent between devices are 32-bit elements; how exact they have to be, the bound alone decides.
No kernel may reach another device: no remote copies, remote signals or barrier semaphores. Data moves between devices by JAX's collectives and lax.ppermute only.
A program may use at most 64 MiB of HBM per device.

v0:
```python
import jax
import jax.numpy as jnp
from jax import lax
from jax.sharding import PartitionSpec as P

EDGE = 8


top_precision = lax.Precision.HIGHEST


def padded(block, sides, width):
    for axis, dim in sides:
        count = lax.axis_size(axis)
        forward = [(i, i + 1) for i in range(count - 1)]
        forward.append((count - 1, 0))
        backward = [(target, source) for source, target in forward]
        low = lax.ppermute(
            lax.slice_in_dim(block, block.shape[dim] - width, None, axis=dim), axis, forward
        )
        high = lax.ppermute(lax.slice_in_dim(block, 0, width, axis=dim), axis, backward)
        block = jnp.concatenate([low, block, high], axis=dim)
    return block


def node_points():
    node_index = jnp.arange(EDGE).astype(jnp.float32)
    return -jnp.cos(jnp.pi * node_index / (EDGE - 1))


def derivative_matrix():
    points = node_points()
    node_index = jnp.arange(EDGE)
    weights = jnp.where((node_index == 0) | (node_index == EDGE - 1), 2.0, 1.0).astype(jnp.float32)
    parity = jnp.where((node_index[:, None] + node_index[None, :]) % 2 == 0, 1.0, -1.0).astype(
        jnp.float32
    )
    identity = jnp.eye(EDGE, dtype=jnp.float32)
    spacing = points[:, None] - points[None, :] + identity
    offdiag = weights[:, None] / weights[None, :] * parity / spacing * (1.0 - identity)
    return offdiag - jnp.diag(jnp.sum(offdiag, axis=1))


def corner_table():
    points = node_points()
    hat_values = jnp.stack([(1.0 - points) * 0.5, (1.0 + points) * 0.5])
    corner_weights = (
        hat_values[:, None, None, :, None, None]
        * hat_values[None, :, None, None, :, None]
        * hat_values[None, None, :, None, None, :]
    )
    return corner_weights.reshape(8, EDGE**3)


def contract(matrices, element_cube, axis):
    moved = jnp.moveaxis(element_cube, axis, 0)
    total = matrices[0][:, None, None, :] * moved[0][None]
    for index in range(1, EDGE):
        total = total + matrices[index][:, None, None, :] * moved[index][None]
    return jnp.moveaxis(total, 0, axis)


def orient_columns(face_cols, orient_codes):
    face_grid = face_cols.reshape(EDGE, EDGE, -1)
    face_grid = jnp.where((orient_codes % 2 == 1)[None, None, :], face_grid[::-1, :, :], face_grid)
    face_grid = jnp.where(
        (orient_codes // 2 % 2 == 1)[None, None, :], face_grid[:, ::-1, :], face_grid
    )
    face_grid = jnp.where(
        (orient_codes >= 4)[None, None, :], jnp.swapaxes(face_grid, 0, 1), face_grid
    )
    return face_grid.reshape(EDGE * EDGE, -1)


def fdm_solve(element_cube, vectors, values):
    spectral = contract(vectors[0], element_cube, 0)
    spectral = contract(vectors[1], spectral, 1)
    spectral = contract(vectors[2], spectral, 2)
    eigen_sums = (
        values[0][:, None, None, :] + values[1][None, :, None, :] + values[2][None, None, :, :]
    )
    spectral = spectral / eigen_sums
    restored = contract(jnp.swapaxes(vectors[0], 0, 1), spectral, 0)
    restored = contract(jnp.swapaxes(vectors[1], 0, 1), restored, 1)
    return contract(jnp.swapaxes(vectors[2], 0, 1), restored, 2)


def local_operator(field, diag_part, cross_part, derivative):
    element_cube = field.reshape(EDGE, EDGE, EDGE, -1)
    diagonal = diag_part.astype(jnp.float32).reshape(3, EDGE, EDGE, EDGE, -1)
    cross_terms = cross_part.astype(jnp.float32).reshape(3, EDGE, EDGE, EDGE, -1)
    forward = jnp.transpose(derivative)[:, :, None]
    backward = derivative[:, :, None]
    grad_first = contract(forward, element_cube, 0)
    grad_second = contract(forward, element_cube, 1)
    grad_third = contract(forward, element_cube, 2)
    flux_first = (
        diagonal[0] * grad_first + cross_terms[0] * grad_second + cross_terms[1] * grad_third
    )
    flux_second = (
        cross_terms[0] * grad_first + diagonal[1] * grad_second + cross_terms[2] * grad_third
    )
    flux_third = (
        cross_terms[1] * grad_first + cross_terms[2] * grad_second + diagonal[2] * grad_third
    )
    curvature = jnp.sum(
        grad_first * flux_first + grad_second * flux_second + grad_third * flux_third
    ) + jnp.sum(element_cube * element_cube)
    applied = contract(backward, flux_first, 0)
    applied = applied + contract(backward, flux_second, 1)
    applied = applied + contract(backward, flux_third, 2)
    return ((applied + element_cube).reshape(EDGE**3, -1), curvature)


def face_sum(field, section_face, section_code, pipe_face, pipe_code):
    element_cube = field.reshape(EDGE, EDGE, EDGE, -1)
    slot_count = element_cube.shape[3]
    stacked = jnp.stack(
        [
            element_cube[0],
            element_cube[EDGE - 1],
            element_cube[:, 0],
            element_cube[:, EDGE - 1],
            element_cube[:, :, 0],
            element_cube[:, :, EDGE - 1],
        ],
        axis=-1,
    )
    face_values = stacked.reshape(EDGE * EDGE, slot_count * 6)
    face_count = face_values.shape[1]
    peer_count = section_face.shape[1]
    capacity = section_face.shape[2]
    wanted = section_face[0].reshape(-1)
    picked = jnp.take(face_values, jnp.maximum(wanted, 0), axis=1)
    outgoing = jnp.where((wanted >= 0)[None, :], picked, 0.0).reshape(
        EDGE * EDGE, peer_count, capacity
    )
    own_index = lax.axis_index("gy")
    arrived = lax.all_to_all(outgoing, "gy", split_axis=1, concat_axis=1, tiled=True)
    swapped = arrived.reshape(EDGE * EDGE, peer_count, capacity // 2, 2)[..., ::-1].reshape(
        EDGE * EDGE, peer_count, capacity
    )
    arrived = jnp.where((jnp.arange(peer_count) == own_index)[None, :, None], swapped, arrived)
    incoming = orient_columns(
        arrived.reshape(EDGE * EDGE, peer_count * capacity), section_code[0].reshape(-1)
    )
    pipe_ids = pipe_face[0]
    pipe_width = pipe_ids.shape[1]
    boundary = jnp.take(face_values, pipe_ids.reshape(-1), axis=1).reshape(
        EDGE * EDGE, 2, pipe_width
    )
    extended = padded(boundary, (("gx", 1),), 1)
    beside = jnp.concatenate([extended[:, 0], extended[:, 3]], axis=1)
    beside = orient_columns(beside, pipe_code[0].reshape(-1))
    targets = jnp.concatenate([wanted, pipe_ids.reshape(-1)])
    placed = jnp.where(targets < 0, face_count, targets)
    face_extra = (
        jnp.zeros((EDGE * EDGE, face_count), jnp.float32)
        .at[:, placed]
        .add(jnp.concatenate([incoming, beside], axis=1), mode="drop")
    )
    face_parts = face_extra.reshape(EDGE, EDGE, slot_count, 6)
    element_cube = element_cube.at[0].add(face_parts[..., 0])
    element_cube = element_cube.at[EDGE - 1].add(face_parts[..., 1])
    element_cube = element_cube.at[:, 0].add(face_parts[..., 2])
    element_cube = element_cube.at[:, EDGE - 1].add(face_parts[..., 3])
    element_cube = element_cube.at[:, :, 0].add(face_parts[..., 4])
    element_cube = element_cube.at[:, :, EDGE - 1].add(face_parts[..., 5])
    return element_cube.reshape(EDGE**3, -1)


def on_device(
    solution,
    residual,
    metric_diag,
    metric_cross,
    fdm_vectors,
    fdm_values,
    vertex_ids,
    coarse_inverse,
    elem_live,
    section_face,
    section_code,
    pipe_face,
    pipe_code,
):
    slot_count = residual.shape[1]
    alive_mask = (jnp.arange(slot_count) < elem_live[0]).astype(jnp.float32)
    rmask = residual * alive_mask[None, :]
    corner_weights = corner_table()
    derivative = derivative_matrix()
    corners = jnp.dot(corner_weights, rmask, precision=top_precision)
    coarse_partial = jax.ops.segment_sum(
        corners.reshape(-1), vertex_ids.reshape(-1), num_segments=coarse_inverse.shape[1]
    )
    coarse_rhs = lax.psum(coarse_partial, ("gx", "gy"))
    own_values = jnp.dot(coarse_inverse, coarse_rhs, precision=top_precision)
    coarse_sol = lax.all_gather(own_values, ("gx", "gy"), axis=0, tiled=True)
    smooth = fdm_solve(rmask.reshape(EDGE, EDGE, EDGE, -1), fdm_vectors, fdm_values).reshape(
        EDGE**3, -1
    )
    summed = face_sum(smooth, section_face, section_code, pipe_face, pipe_code)
    lifted = jnp.dot(corner_weights.T, coarse_sol[vertex_ids], precision=top_precision)
    direction = alive_mask[None, :] * (summed + lifted)
    applied, curvature_local = local_operator(direction, metric_diag, metric_cross, derivative)
    image = face_sum(applied, section_face, section_code, pipe_face, pipe_code)
    precond_local = jnp.sum(rmask * direction)
    norm_local = jnp.sum(rmask * rmask)
    precond_dot, curvature, old_norm = lax.psum(
        (precond_local, curvature_local, norm_local), ("gx", "gy")
    )
    step_length = precond_dot / curvature
    residual_out = rmask - step_length * image
    fresh_norm = lax.psum(jnp.sum(residual_out * residual_out), ("gx", "gy"))
    solution_out = alive_mask[None, :] * (solution + step_length * direction)
    norm_ratio = (fresh_norm / old_norm).reshape(1)
    return (solution_out, residual_out, norm_ratio)


def solution(mesh):
    placed = (
        P(None, ("gx", "gy")),
        P(None, ("gx", "gy")),
        P(None, None, ("gx", "gy")),
        P(None, None, ("gx", "gy")),
        P(None, None, None, ("gx", "gy")),
        P(None, None, ("gx", "gy")),
        P(None, ("gx", "gy")),
        P(("gx", "gy"), None),
        P(("gx", "gy")),
        P(("gx", "gy"), None, None),
        P(("gx", "gy"), None, None),
        P(("gx", "gy"), None, None),
        P(("gx", "gy"), None, None),
    )
    return jax.shard_map(
        on_device,
        mesh=mesh,
        in_specs=placed,
        out_specs=(P(None, ("gx", "gy")), P(None, ("gx", "gy")), P()),
        check_vma=False,
    )
```

profile of v0, /device:TPU:0, one launch (start us, length us, event | category | flops | bytes accessed | tf_op | source)
XLA Modules:
  0.0 308.1 jit_solution(1629488625841701484)
XLA Ops:
  0.7 0.9 slice_bitcast_fusion.120
  1.5 0.8 slice_bitcast_fusion.98
  2.3 0.8 slice_bitcast_fusion.92
  3.8 1.0 broadcast_multiply_fusion.3
  11.0 2.0 copy.389
  13.1 1.6 reshape.1869
  14.6 0.8 max.8
  15.4 0.8 reshape_squeeze.8
  16.2 0.8 reshape_squeeze.6
  17.0 0.7 ge.39
  17.8 1.6 gather_fusion.1
  20.2 5.2 %all-to-all-start = ((f32[4,1,1280]{2,1,0:T(1,128)}), f32[4,1,1280]{2,1,0:T(1,128)S(1)}, u32[]{:S(2)}, u32[]{:S(2)}) async-start(f32[4,1,1280]{2,1,0:T(1,128)} %reshape.1990), calls=%async_computation | async-start | bytes 40960 | tf_op jit(solution)/shard_map/all_to_all | solution.py:139
  25.4 1.6 gather_fusion.2
  27.0 0.8 reshape_squeeze.7
  28.2 3.6 %collective-permute-start.1 = (f32[64,1,64]{2,0,1:T(8,128)S(1)}, f32[64,1,64]{2,0,1:T(8,128)S(1)}, u32[]{:S(2)}, u32[]{:S(2)}) collective-permute-start(f32[64,1,64]{2,0,1:T(8,128)S(1)} %copy.455), channel_id=1, source_target_pairs={{4,0},{8,4},{12,8},{16,12},{20,16},{24,20},{28,24},{0,28},{5,1},{9... | collective-permute-start | bytes 49160 | tf_op jit(solution)/shard_map/ppermute | solution.py:21
  31.8 0.8 concatenate.68
  32.6 0.8 multiply_add_fusion.4
  33.3 0.7 broadcast_multiply_fusion.2
  34.8 0.7 fusion.38
  35.5 7.7 %scatter_custom_fusion.1 = f32[512]{0:T(512)S(1)} fusion(s32[1024]{0:T(1024)} %bitcast.651, f32[1024]{0:T(1024)S(1)} %convolution_bitcast_fusion, f32[]{:T(128)} %constant.402.clone.1), kind=kCustom, calls=%fused_computation.285 | custom fusion | flops 1024 | bytes 2560 | tf_op jit(solution)/shard_map/scatter-add | solution.py:193
  43.2 39.2 %psum.35 = f32[512]{0:T(512)S(1)} all-reduce(f32[512]{0:T(512)S(1)} %scatter_custom_fusion.1), channel_id=1, replica_groups=mesh['gx'=8,'gy'=4] {'gx','gy'}, use_global_device_ids=true, to_apply=%region_2.5 | all-reduce | flops 512 | bytes 4096 | tf_op jit(solution)/shard_map/psum | solution.py:196
  82.7 0.9 fusion.55
  83.7 0.9 fusion.54
  88.8 0.9 convert_element_type.56
  89.7 0.9 convert_element_type.57
  108.0 40.6 %all-reduce = f32[512]{0:T(512)S(1)} all-reduce(f32[512]{0:T(512)S(1)} %dynamic-update-slice.36), channel_id=1, replica_groups=mesh['gx'=8,'gy'=4] {'gx','gy'}, use_global_device_ids=true, to_apply=%add | all-reduce | flops 512 | bytes 4096
  148.5 6.9 %gather_fusion = f32[1024]{0:T(1024)S(1)} fusion(f32[512]{0:T(512)S(1)} %all-reduce, s32[1024]{0:T(1024)S(1)} %fusion.38), kind=kCustom, calls=%fused_computation.4 | custom fusion | bytes 12288 | tf_op jit(solution)/shard_map/gather | solution.py:203
  157.5 2.0 scatter_custom_fusion
  159.5 1.9 reshape.1876
  161.5 1.7 fusion.53
  163.2 1.3 copy.456
  164.5 1.2 copy.457
  165.8 1.3 copy.401
  167.1 1.2 copy.403
  168.3 1.2 copy.458
  169.8 0.8 fusion.22
  171.2 1.3 multiply_reduce_fusion
  179.9 2.0 copy.428
  182.0 1.6 reshape.1886
  183.6 1.8 gather_fusion.3
  185.4 1.8 gather_fusion.4
  188.0 4.4 %all-to-all-start.1 = ((f32[4,1,1280]{2,1,0:T(1,128)}), f32[4,1,1280]{2,1,0:T(1,128)S(1)}, u32[]{:S(2)}, u32[]{:S(2)}) async-start(f32[4,1,1280]{2,1,0:T(1,128)} %reshape.1992), calls=%async_computation.1 | async-start | bytes 40960 | tf_op jit(solution)/shard_map/all_to_all | solution.py:139
  192.8 3.6 %collective-permute-start.3 = (f32[64,1,64]{2,0,1:T(8,128)S(1)}, f32[64,1,64]{2,0,1:T(8,128)S(1)}, u32[]{:S(2)}, u32[]{:S(2)}) collective-permute-start(f32[64,1,64]{2,0,1:T(8,128)S(1)} %copy.461), channel_id=1, source_target_pairs={{4,0},{8,4},{12,8},{16,12},{20,16},{24,20},{28,24},{0,28},{5,1},{9... | collective-permute-start | bytes 49160 | tf_op jit(solution)/shard_map/ppermute | solution.py:21
  196.3 0.8 mul.2629
  197.1 0.8 mul.2637
  197.9 0.8 mul.2645
  198.9 0.9 mul.2653
  199.8 0.8 mul.2661
  200.5 0.8 mul.2669
  201.3 0.8 mul.2677
  203.1 2.9 add_reduce_fusion
  207.2 38.8 %all-reduce.2 = (f32[]{:T(128)}, f32[]{:T(128)}) all-reduce(f32[]{:T(128)} %get-tuple-element.150, f32[]{:T(128)S(6)} %add.970), channel_id=1, replica_groups=mesh['gx'=8,'gy'=4] {'gx','gy'}, use_global_device_ids=true, to_apply=%region_4.7 | all-reduce | flops 2 | bytes 16 | tf_op jit(solution)/shard_map/psum | solution.py:209
  247.3 0.7 add_multiply_fusion
  248.0 0.7 reduce.27
  249.7 2.1 scatter_custom_fusion.2
  251.8 1.9 reshape.1893
  253.7 1.7 fusion.52
  255.4 1.3 copy.462
  256.7 1.2 copy.463
  258.0 1.2 copy.440
  259.4 1.2 copy.442
  260.8 1.2 copy.464
  262.4 1.3 multiply_reduce_fusion.1
  263.8 41.8 %all-reduce.1 = (f32[]{:T(128)}, f32[]{:T(128)}) all-reduce(f32[]{:T(128)} %get-tuple-element.156, f32[]{:T(128)} %get-tuple-element.149), channel_id=1, replica_groups=mesh['gx'=8,'gy'=4] {'gx','gy'}, use_global_device_ids=true, to_apply=%region_11.14 | all-reduce | flops 2 | bytes 16 | tf_op jit(solution)/shard_map/psum | solution.py:214
  (507 shorter events, 42.4 us)
Async XLA Ops:
  0.6 84.6 %copy-start = (f32[16,512]{1,0:T(8,128)S(1)}, f32[16,512]{1,0:T(8,128)}, u32[]{:S(2)}) copy-start(f32[16,512]{1,0:T(8,128)} %param.48) | copy-start | bytes 98308
  4.7 29.8 %copy-start.1 = (f32[512,128]{1,0:T(8,128)}, f32[512,128]{1,0:T(8,128)S(1)}, u32[]{:S(2)}) copy-start(f32[512,128]{1,0:T(8,128)S(1)} %broadcast_multiply_fusion.3) | copy-start | bytes 786436
  14.6 68.1 %copy-start.4 = (bf16[3,512,128]{2,1,0:T(8,128)(2,1)S(1)}, bf16[3,512,128]{2,1,0:T(8,128)(2,1)}, u32[]{:S(2)}) copy-start(bf16[3,512,128]{2,1,0:T(8,128)(2,1)} %param.44) | copy-start | bytes 1179652
  14.6 69.0 %copy-start.3 = (bf16[3,512,128]{2,1,0:T(8,128)(2,1)S(1)}, bf16[3,512,128]{2,1,0:T(8,128)(2,1)}, u32[]{:S(2)}) copy-start(bf16[3,512,128]{2,1,0:T(8,128)(2,1)} %param.43) | copy-start | bytes 1179652
  17.0 140.1 %copy-start.78 = (pred[80]{0:T(512)(128)(4,1)}, pred[80]{0:T(512)(128)(4,1)S(1)}, u32[]{:S(2)}) copy-start(pred[80]{0:T(512)(128)(4,1)S(1)} %get-tuple-element.357) | copy-start | bytes 244
  17.0 140.1 %copy-start.95 = (pred[80]{0:T(512)(128)(4,1)}, pred[80]{0:T(512)(128)(4,1)S(1)}, u32[]{:S(2)}) copy-start(pred[80]{0:T(512)(128)(4,1)S(1)} %get-tuple-element.358) | copy-start | bytes 244
  17.0 140.1 %copy-start.125 = (pred[80]{0:T(512)(128)(4,1)}, pred[80]{0:T(512)(128)(4,1)S(1)}, u32[]{:S(2)}) copy-start(pred[80]{0:T(512)(128)(4,1)S(1)} %get-tuple-element.356) | copy-start | bytes 244
  17.8 9.3 %copy-start.135 = (pred[80]{0:T(512)(128)(4,1)}, pred[80]{0:T(512)(128)(4,1)S(1)}, u32[]{:S(2)}) copy-start(pred[80]{0:T(512)(128)(4,1)S(1)} %ge.39) | copy-start | bytes 244
  17.8 9.2 %copy-start.123 = (s32[1024]{0:T(1024)}, s32[1024]{0:T(1024)S(1)}, u32[]{:S(2)}) copy-start(s32[1024]{0:T(1024)S(1)} %get-tuple-element.373) | copy-start | bytes 12292
  20.2 135.2 %all-to-all-start = ((f32[4,1,1280]{2,1,0:T(1,128)}), f32[4,1,1280]{2,1,0:T(1,128)S(1)}, u32[]{:S(2)}, u32[]{:S(2)}) async-start(f32[4,1,1280]{2,1,0:T(1,128)} %reshape.1990), calls=%async_computation | async-start | bytes 40960 | tf_op jit(solution)/shard_map/all_to_all | solution.py:139
  27.8 129.4 %copy-start.80 = (pred[128]{0:T(512)(128)(4,1)}, pred[128]{0:T(512)(128)(4,1)S(1)}, u32[]{:S(2)}) copy-start(pred[128]{0:T(512)(128)(4,1)S(1)} %get-tuple-element.360) | copy-start | bytes 388
  27.9 129.4 %copy-start.97 = (pred[128]{0:T(512)(128)(4,1)}, pred[128]{0:T(512)(128)(4,1)S(1)}, u32[]{:S(2)}) copy-start(pred[128]{0:T(512)(128)(4,1)S(1)} %get-tuple-element.361) | copy-start | bytes 388
  27.9 129.5 %copy-start.127 = (pred[128]{0:T(512)(128)(4,1)}, pred[128]{0:T(512)(128)(4,1)S(1)}, u32[]{:S(2)}) copy-start(pred[128]{0:T(512)(128)(4,1)S(1)} %get-tuple-element.359) | copy-start | bytes 388
  28.1 129.1 %collective-permute-start = (f32[64,1,64]{2,0,1:T(8,128)S(1)}, f32[64,1,64]{2,0,1:T(8,128)S(1)}, u32[]{:S(2)}, u32[]{:S(2)}) collective-permute-start(f32[64,1,64]{2,0,1:T(8,128)S(1)} %copy.454), channel_id=1, source_target_pairs={{0,4},{4,8},{8,12},{12,16},{16,20},{20,24},{24,28},{28,0},{1,5},{5... | collective-permute-start | bytes 49160 | tf_op jit(solution)/shard_map/ppermute | solution.py:18
  28.2 129.0 %collective-permute-start.1 = (f32[64,1,64]{2,0,1:T(8,128)S(1)}, f32[64,1,64]{2,0,1:T(8,128)S(1)}, u32[]{:S(2)}, u32[]{:S(2)}) collective-permute-start(f32[64,1,64]{2,0,1:T(8,128)S(1)} %copy.455), channel_id=1, source_target_pairs={{4,0},{8,4},{12,8},{16,12},{20,16},{24,20},{28,24},{0,28},{5,1},{9... | collective-permute-start | bytes 49160 | tf_op jit(solution)/shard_map/ppermute | solution.py:21
  82.7 20.4 %copy-start.66 = (f32[8]{0:T(128)}, f32[8]{0:T(128)S(1)}, u32[]{:S(2)}) copy-start(f32[8]{0:T(128)S(1)} %get-tuple-element.353) | copy-start | bytes 100
  82.7 21.1 %copy-start.64 = (f32[8]{0:T(128)}, f32[8]{0:T(128)S(1)}, u32[]{:S(2)}) copy-start(f32[8]{0:T(128)S(1)} %get-tuple-element.352) | copy-start | bytes 100
  82.7 21.8 %copy-start.62 = (f32[8]{0:T(128)}, f32[8]{0:T(128)S(1)}, u32[]{:S(2)}) copy-start(f32[8]{0:T(128)S(1)} %get-tuple-element.351) | copy-start | bytes 100
  82.7 22.4 %copy-start.60 = (f32[8]{0:T(128)}, f32[8]{0:T(128)S(1)}, u32[]{:S(2)}) copy-start(f32[8]{0:T(128)S(1)} %get-tuple-element.350) | copy-start | bytes 100
  85.2 72.3 %copy-start.137 = (s32[208,1]{0,1:T(1,128)}, s32[208,1]{0,1:T(1,128)S(1)}, u32[]{:S(2)}) copy-start(s32[208,1]{0,1:T(1,128)S(1)} %compare_select_fusion.1) | copy-start | bytes 2500
  85.4 71.4 %copy-start.133 = (pred[4]{0:T(512)(128)(4,1)}, pred[4]{0:T(512)(128)(4,1)S(1)}, u32[]{:S(2)}) copy-start(pred[4]{0:T(512)(128)(4,1)S(1)} %iota_compare_fusion.2) | copy-start | bytes 16
  163.2 6.6 %copy-start.73 = (f32[1,8,128]{2,0,1:T(1,128)S(1)}, f32[1,8,128]{2,0,1:T(1,128)}, u32[]{:S(2)}) copy-start(f32[1,8,128]{2,0,1:T(1,128)} %copy-done.72) | copy-start | bytes 12292
  163.2 6.6 %copy-start.75 = (f32[1,8,128]{2,0,1:T(1,128)S(1)}, f32[1,8,128]{2,0,1:T(1,128)}, u32[]{:S(2)}) copy-start(f32[1,8,128]{2,0,1:T(1,128)} %copy-done.74) | copy-start | bytes 12292
  163.2 6.6 %copy-start.77 = (f32[1,8,128]{2,0,1:T(1,128)S(1)}, f32[1,8,128]{2,0,1:T(1,128)}, u32[]{:S(2)}) copy-start(f32[1,8,128]{2,0,1:T(1,128)} %copy-done.76) | copy-start | bytes 12292
  163.2 8.0 %copy-start.2 = (f32[512,128]{1,0:T(8,128)S(1)}, f32[512,128]{1,0:T(8,128)}, u32[]{:S(2)}) copy-start(f32[512,128]{1,0:T(8,128)} %copy-done.1) | copy-start | bytes 786436
  163.2 8.0 %copy-start.85 = (f32[128]{0:T(128)S(1)}, f32[128]{0:T(128)}, u32[]{:S(2)}) copy-start(f32[128]{0:T(128)} %copy-done.84) | copy-start | bytes 1540
  165.7 7.2 %copy-start.11 = (f32[1,512,128]{2,1,0:T(8,128)S(1)}, f32[1,512,128]{2,1,0:T(8,128)}, u32[]{:S(2)}) copy-start(f32[1,512,128]{2,1,0:T(8,128)} %get-tuple-element.174) | copy-start | bytes 786436
  165.7 7.2 %copy-start.13 = (f32[1,512,128]{2,1,0:T(8,128)S(1)}, f32[1,512,128]{2,1,0:T(8,128)}, u32[]{:S(2)}) copy-start(f32[1,512,128]{2,1,0:T(8,128)} %get-tuple-element.173) | copy-start | bytes 786436
  165.7 7.2 %copy-start.18 = (f32[1,512,128]{2,1,0:T(8,128)S(1)}, f32[1,512,128]{2,1,0:T(8,128)}, u32[]{:S(2)}) copy-start(f32[1,512,128]{2,1,0:T(8,128)} %get-tuple-element.170) | copy-start | bytes 786436
  165.8 7.2 %copy-start.61 = (f32[8]{0:T(128)S(1)}, f32[8]{0:T(128)}, u32[]{:S(2)}) copy-start(f32[8]{0:T(128)} %copy-done.60) | copy-start | bytes 100
  165.8 7.2 %copy-start.63 = (f32[8]{0:T(128)S(1)}, f32[8]{0:T(128)}, u32[]{:S(2)}) copy-start(f32[8]{0:T(128)} %copy-done.62) | copy-start | bytes 100
  165.8 7.2 %copy-start.65 = (f32[8]{0:T(128)S(1)}, f32[8]{0:T(128)}, u32[]{:S(2)}) copy-start(f32[8]{0:T(128)} %copy-done.64) | copy-start | bytes 100
  165.8 7.2 %copy-start.67 = (f32[8]{0:T(128)S(1)}, f32[8]{0:T(128)}, u32[]{:S(2)}) copy-start(f32[8]{0:T(128)} %copy-done.66) | copy-start | bytes 100
  179.9 7.3 %copy-start.132 = (pred[80]{0:T(512)(128)(4,1)S(1)}, pred[80]{0:T(512)(128)(4,1)}, u32[]{:S(2)}) copy-start(pred[80]{0:T(512)(128)(4,1)} %copy-done.131) | copy-start | bytes 244
  179.9 7.3 %copy-start.136 = (pred[80]{0:T(512)(128)(4,1)S(1)}, pred[80]{0:T(512)(128)(4,1)}, u32[]{:S(2)}) copy-start(pred[80]{0:T(512)(128)(4,1)} %copy-done.135) | copy-start | bytes 244
  179.9 12.6 %copy-start.130 = (pred[128]{0:T(512)(128)(4,1)S(1)}, pred[128]{0:T(512)(128)(4,1)}, u32[]{:S(2)}) copy-start(pred[128]{0:T(512)(128)(4,1)} %copy-done.129) | copy-start | bytes 388
  183.5 18.5 %copy-start.30 = (f32[8,8,128]{2,1,0:T(8,128)S(1)}, f32[8,8,128]{2,1,0:T(8,128)}, u32[]{:S(2)}) copy-start(f32[8,8,128]{2,1,0:T(8,128)} %copy-done.29) | copy-start | bytes 98308
  183.5 18.6 %copy-start.53 = (f32[8,8,128]{2,1,0:T(8,128)S(1)}, f32[8,8,128]{2,1,0:T(8,128)}, u32[]{:S(2)}) copy-start(f32[8,8,128]{2,1,0:T(8,128)} %copy-done.52) | copy-start | bytes 98308
  183.5 18.6 %copy-start.51 = (f32[8,8,128]{2,1,0:T(8,128)S(1)}, f32[8,8,128]{2,1,0:T(8,128)}, u32[]{:S(2)}) copy-start(f32[8,8,128]{2,1,0:T(8,128)} %copy-done.50) | copy-start | bytes 98308
  183.6 18.7 %copy-start.49 = (f32[8,8,128]{2,1,0:T(8,128)S(1)}, f32[8,8,128]{2,1,0:T(8,128)}, u32[]{:S(2)}) copy-start(f32[8,8,128]{2,1,0:T(8,128)} %copy-done.48) | copy-start | bytes 98308
  183.6 18.7 %copy-start.46 = (f32[8,8,128]{2,1,0:T(8,128)S(1)}, f32[8,8,128]{2,1,0:T(8,128)}, u32[]{:S(2)}) copy-start(f32[8,8,128]{2,1,0:T(8,128)} %copy-done.45) | copy-start | bytes 98308
  183.6 18.8 %copy-start.43 = (f32[8,8,128]{2,1,0:T(8,128)S(1)}, f32[8,8,128]{2,1,0:T(8,128)}, u32[]{:S(2)}) copy-start(f32[8,8,128]{2,1,0:T(8,128)} %copy-done.42) | copy-start | bytes 98308
  183.6 18.8 %copy-start.40 = (f32[8,8,128]{2,1,0:T(8,128)S(1)}, f32[8,8,128]{2,1,0:T(8,128)}, u32[]{:S(2)}) copy-start(f32[8,8,128]{2,1,0:T(8,128)} %copy-done.39) | copy-start | bytes 98308
  183.6 18.8 %copy-start.37 = (f32[8,8,128]{2,1,0:T(8,128)S(1)}, f32[8,8,128]{2,1,0:T(8,128)}, u32[]{:S(2)}) copy-start(f32[8,8,128]{2,1,0:T(8,128)} %copy-done.36) | copy-start | bytes 98308
  183.6 18.9 %copy-start.34 = (f32[8,8,128]{2,1,0:T(8,128)S(1)}, f32[8,8,128]{2,1,0:T(8,128)}, u32[]{:S(2)}) copy-start(f32[8,8,128]{2,1,0:T(8,128)} %copy-done.33) | copy-start | bytes 98308
  183.6 18.9 %copy-start.28 = (f32[1,8,8,128]{3,0,2,1:T(1,128)S(1)}, f32[1,8,8,128]{3,0,2,1:T(1,128)}, u32[]{:S(2)}) copy-start(f32[1,8,8,128]{3,0,2,1:T(1,128)} %copy-done.27) | copy-start | bytes 98308
  183.6 18.9 %copy-start.26 = (f32[1,8,8,128]{3,0,2,1:T(1,128)S(1)}, f32[1,8,8,128]{3,0,2,1:T(1,128)}, u32[]{:S(2)}) copy-start(f32[1,8,8,128]{3,0,2,1:T(1,128)} %copy-done.25) | copy-start | bytes 98308
  185.4 17.1 %copy-start.24 = (f32[1,8,8,128]{3,0,2,1:T(1,128)S(1)}, f32[1,8,8,128]{3,0,2,1:T(1,128)}, u32[]{:S(2)}) copy-start(f32[1,8,8,128]{3,0,2,1:T(1,128)} %copy-done.23) | copy-start | bytes 98308
  187.2 15.4 %copy-start.22 = (f32[1,8,8,128]{3,0,2,1:T(1,128)S(1)}, f32[1,8,8,128]{3,0,2,1:T(1,128)}, u32[]{:S(2)}) copy-start(f32[1,8,8,128]{3,0,2,1:T(1,128)} %copy-done.21) | copy-start | bytes 98308
  188.0 60.0 %all-to-all-start.1 = ((f32[4,1,1280]{2,1,0:T(1,128)}), f32[4,1,1280]{2,1,0:T(1,128)S(1)}, u32[]{:S(2)}, u32[]{:S(2)}) async-start(f32[4,1,1280]{2,1,0:T(1,128)} %reshape.1992), calls=%async_computation.1 | async-start | bytes 40960 | tf_op jit(solution)/shard_map/all_to_all | solution.py:139
  192.5 10.1 %copy-start.20 = (f32[1,8,8,128]{3,0,2,1:T(1,128)S(1)}, f32[1,8,8,128]{3,0,2,1:T(1,128)}, u32[]{:S(2)}) copy-start(f32[1,8,8,128]{3,0,2,1:T(1,128)} %copy-done.19) | copy-start | bytes 98308
  192.7 56.6 %collective-permute-start.2 = (f32[64,1,64]{2,0,1:T(8,128)S(1)}, f32[64,1,64]{2,0,1:T(8,128)S(1)}, u32[]{:S(2)}, u32[]{:S(2)}) collective-permute-start(f32[64,1,64]{2,0,1:T(8,128)S(1)} %copy.460), channel_id=1, source_target_pairs={{0,4},{4,8},{8,12},{12,16},{16,20},{20,24},{24,28},{28,0},{1,5},{5... | collective-permute-start | bytes 49160 | tf_op jit(solution)/shard_map/ppermute | solution.py:18
  192.8 56.5 %collective-permute-start.3 = (f32[64,1,64]{2,0,1:T(8,128)S(1)}, f32[64,1,64]{2,0,1:T(8,128)S(1)}, u32[]{:S(2)}, u32[]{:S(2)}) collective-permute-start(f32[64,1,64]{2,0,1:T(8,128)S(1)} %copy.461), channel_id=1, source_target_pairs={{4,0},{8,4},{12,8},{16,12},{20,16},{24,20},{28,24},{0,28},{5,1},{9... | collective-permute-start | bytes 49160 | tf_op jit(solution)/shard_map/ppermute | solution.py:21
  203.0 44.3 %copy-start.54 = (f32[512,128]{1,0:T(8,128)S(1)}, f32[512,128]{1,0:T(8,128)}, u32[]{:S(2)}) copy-start(f32[512,128]{1,0:T(8,128)} %param.41) | copy-start | bytes 786436
  203.0 44.3 %copy-start.86 = (f32[128]{0:T(128)S(1)}, f32[128]{0:T(128)}, u32[]{:S(2)}) copy-start(f32[128]{0:T(128)} %copy-done.84) | copy-start | bytes 1540
  203.0 45.8 %copy-start.134 = (pred[4]{0:T(512)(128)(4,1)S(1)}, pred[4]{0:T(512)(128)(4,1)}, u32[]{:S(2)}) copy-start(pred[4]{0:T(512)(128)(4,1)} %copy-done.133) | copy-start | bytes 16
  203.0 46.2 %copy-start.79 = (pred[80]{0:T(512)(128)(4,1)S(1)}, pred[80]{0:T(512)(128)(4,1)}, u32[]{:S(2)}) copy-start(pred[80]{0:T(512)(128)(4,1)} %copy-done.78) | copy-start | bytes 244
  203.0 46.2 %copy-start.96 = (pred[80]{0:T(512)(128)(4,1)S(1)}, pred[80]{0:T(512)(128)(4,1)}, u32[]{:S(2)}) copy-start(pred[80]{0:T(512)(128)(4,1)} %copy-done.95) | copy-start | bytes 244
  203.1 46.2 %copy-start.126 = (pred[80]{0:T(512)(128)(4,1)S(1)}, pred[80]{0:T(512)(128)(4,1)}, u32[]{:S(2)}) copy-start(pred[80]{0:T(512)(128)(4,1)} %copy-done.125) | copy-start | bytes 244
  203.1 46.3 %copy-start.81 = (pred[128]{0:T(512)(128)(4,1)S(1)}, pred[128]{0:T(512)(128)(4,1)}, u32[]{:S(2)}) copy-start(pred[128]{0:T(512)(128)(4,1)} %copy-done.80) | copy-start | bytes 388
  203.1 46.3 %copy-start.98 = (pred[128]{0:T(512)(128)(4,1)S(1)}, pred[128]{0:T(512)(128)(4,1)}, u32[]{:S(2)}) copy-start(pred[128]{0:T(512)(128)(4,1)} %copy-done.97) | copy-start | bytes 388
  203.1 46.4 %copy-start.128 = (pred[128]{0:T(512)(128)(4,1)S(1)}, pred[128]{0:T(512)(128)(4,1)}, u32[]{:S(2)}) copy-start(pred[128]{0:T(512)(128)(4,1)} %copy-done.127) | copy-start | bytes 388
  255.4 6.6 %copy-start.14 = (f32[8,8,128,1]{1,0,3,2:T(8,128)S(1)}, f32[8,8,128,1]{1,0,3,2:T(8,128)}, u32[]{:S(2)}) copy-start(f32[8,8,128,1]{1,0,3,2:T(8,128)} %get-tuple-element.158) | copy-start | bytes 98308
  255.4 7.0 %copy-start.16 = (f32[512,128]{1,0:T(8,128)S(1)}, f32[512,128]{1,0:T(8,128)}, u32[]{:S(2)}) copy-start(f32[512,128]{1,0:T(8,128)} %param.42) | copy-start | bytes 786436
  (80 other events, 251.7 us)
where the time goes:
time: 310 us; the launch traced here: 308 us
  blocking collectives  160 us (52%)
  local copies, waits for them, and re-layouts  89.9 us (29%)
  other arithmetic  30.2 us (10%)
  starting transfers between devices  16.8 us (5%)
  between operations  9.19 us (3%)
    psum x1, blocking collectives, on_device(): fresh_norm = lax.psum(jnp.sum(residual_out * residual_out), ('gx', 'gy'))  41.8 us
    unnamed x1, blocking collectives  40.6 us
    psum x1, blocking collectives, on_device(): coarse_rhs = lax.psum(coarse_partial, ('gx', 'gy'))  39.2 us
    psum x1, blocking collectives, on_device(): lax.psum((precond_local, curvature_local, norm_local), ('gx', 'gy'))  38.8 us
    mul x78, local copies, waits for them, and re-layouts, contract(): total = total + matrices[index][:, None, None, :] * moved[index][None]  20.9 us
    unnamed x304, local copies, waits for them, and re-layouts  16.6 us
    all_to_all x2, starting transfers between devices, face_sum(): lax.all_to_all(outgoing, 'gy', split_axis=1, concat_axis=1, tiled=True)  9.61 us
    another operation x9, local copies, waits for them, and re-layouts  8.32 us
  transfers between devices with their start and end apart: 6, of which 0 were waited for; matrix products, arithmetic and copies ran while one was open for 19% of the time, Pallas kernels for 0%

commit v1 on v0

v1 whole, which is shorter than its diff:
```python
import functools

import jax
import jax.numpy as jnp
import numpy as np
from jax import lax
from jax.experimental import pallas as pl
from jax.experimental.pallas import tpu as pltpu
from jax.sharding import PartitionSpec as P

EDGE = 8
PLANE = EDGE * EDGE
POINTS = EDGE**3
FACES = 6
CORNERS = 8
LANES = 128
AXES = ("gx", "gy")
DIRECT_BYTES = 1 << 20

exact = lax.Precision.HIGHEST
f32 = jnp.float32
bf16 = jnp.bfloat16


def node_tables():
    index = np.arange(EDGE)
    points = -np.cos(np.pi * index / (EDGE - 1))
    ends = np.where((index == 0) | (index == EDGE - 1), 2.0, 1.0)
    derivative = np.zeros((EDGE, EDGE))
    for a in range(EDGE):
        for b in range(EDGE):
            if a != b:
                derivative[a, b] = ends[a] / ends[b] * (-1.0) ** (a + b) / (points[a] - points[b])
    derivative -= np.diag(derivative.sum(axis=1))
    hats = np.stack([(1.0 - points) / 2, (1.0 + points) / 2])
    return derivative, hats


DERIVATIVE, HATS = node_tables()


TALL = POINTS + EDGE


def number(value):
    return float(np.float32(value))


def pairings(count):
    ring = np.arange(count)
    return [ring ^ 1, (((ring + 1) ^ 1) - 1) % count]


def section_pairings(count):
    ring = np.arange(count)
    found = []
    for table in [
        *pairings(count),
        (ring + count // 2) % count,
        ring ^ 2,
        (((ring + 2) ^ 2) - 2) % count,
    ]:
        if not any(np.array_equal(table, other) for other in found):
            found.append(table)
    return found


def chosen(table, own):
    value = jnp.int32(table[0])
    for place in range(1, len(table)):
        value = jnp.where(own == place, jnp.int32(table[place]), value)
    return value


def lane_index(rows=1, width=LANES):
    return lax.broadcasted_iota(jnp.int32, (rows, width), 1)


def halves(values):
    top = values.astype(bf16)
    rest = (values - top.astype(f32)).astype(bf16)
    return jnp.concatenate([top, rest], axis=0)


def joined(product):
    rows = product.shape[0] // 2
    return product[:rows] + product[rows:]


def pad_lanes(row, width, fill):
    if row.shape[1] == width:
        return row
    return jnp.concatenate([row, jnp.full((1, width - row.shape[1]), fill, row.dtype)], axis=1)


def added(members):
    members = list(members)
    while len(members) > 1:
        pairs = [left + right for left, right in zip(members[0::2], members[1::2])]
        members = pairs + members[2 * len(pairs) :]
    return members[0]


def fold(values):
    return added(
        [values[row : row + EDGE] for row in range(0, values.shape[0], EDGE)]
    )


def total_of(values):
    return jnp.sum(jnp.sum(fold(values), axis=0, keepdims=True), axis=1, keepdims=True)


def lane_row(members):
    lanes = lane_index()
    row = jnp.zeros((1, LANES), f32)
    for place, member in enumerate(members):
        row = jnp.where(lanes == place, member, row)
    return row


def begin(copies):
    started = [pltpu.make_async_copy(*copy) for copy in copies]
    for copy in started:
        copy.start()
    return started


def section_row(table_ref, fill):
    peers, capacity = table_ref.shape
    own = lax.axis_index("gy")
    partners = [own] + [chosen(table, own) for table in section_pairings(peers)]
    rows = [table_ref[pl.ds(partner, 1), :] for partner in partners]
    width = -(-len(rows) * capacity // LANES) * LANES
    return pad_lanes(jnp.concatenate(rows, axis=1), width, fill)


def pipe_row(table_ref):
    side = lax.rem(lax.axis_index("gx"), 2)
    return jnp.concatenate(
        [table_ref[pl.ds(1 - side, 1), :], table_ref[pl.ds(side, 1), :]], axis=1
    )


def face_columns(ids, slots):
    element = ids // FACES
    return jnp.where(ids < 0, -1, (ids - element * FACES) * slots + element)


def slot_columns(slots, section_ref, pipe_ref):
    ids = jnp.concatenate([section_row(section_ref, -1), pipe_row(pipe_ref)], axis=1)
    return face_columns(ids, slots)


def slot_codes(section_code_ref, pipe_code_ref):
    codes = jnp.concatenate([section_row(section_code_ref, 0), pipe_row(pipe_code_ref)], axis=1)
    return jnp.broadcast_to(codes, (EDGE, codes.shape[1]))


def one_hot(columns, height):
    rows = lax.broadcasted_iota(jnp.int32, (height, columns.shape[1]), 0)
    return jnp.where(rows == columns, 1.0, 0.0).astype(bf16)


def pick_faces(cube_ref, hot_ref, capacity, section_out, pipe_out):
    last = EDGE - 1
    faces = [
        cube_ref[0:PLANE, :],
        cube_ref[last * PLANE : EDGE * PLANE, :],
        jnp.concatenate([cube_ref[i * PLANE : i * PLANE + EDGE, :] for i in range(EDGE)], axis=0),
        jnp.concatenate(
            [cube_ref[(i + 1) * PLANE - EDGE : (i + 1) * PLANE, :] for i in range(EDGE)], axis=0
        ),
        cube_ref[pl.ds(0, PLANE, stride=EDGE), :],
        cube_ref[pl.ds(last, PLANE, stride=EDGE), :],
    ]
    values = halves(jnp.concatenate(faces, axis=1))
    picked = joined(jnp.dot(values, hot_ref[...], preferred_element_type=f32))
    width = section_out.shape[1]
    pipe_out[...] = picked[:, width:]
    section = picked[:, :width]
    first = section[:, :LANES]
    after = pltpu.roll(first, LANES - 1, axis=1)
    before = pltpu.roll(first, 1, axis=1)
    lanes = lane_index()
    paired = jnp.where(lanes % 2 == 0, after, before)
    section_out[...] = section
    section_out[:, :LANES] = jnp.where(lanes < capacity, paired, first)


def section_columns(capacity, block_refs, order):
    own_ref, *arrived = block_refs
    lanes = lane_index(1, own_ref.shape[1])
    section = own_ref[...]
    for place, member_ref in zip(order, arrived):
        start = (place + 1) * capacity
        section = jnp.where(
            (lanes >= start) & (lanes < start + capacity), member_ref[...], section
        )
    return section


def pipe_columns(first_ref, second_ref):
    half = first_ref.shape[1] // 2
    return jnp.where(lane_index(1, 2 * half) < half, first_ref[...], second_ref[...])


def packed_height(capacity):
    return -(-EDGE // (LANES // capacity)) * EDGE


def pack_section(section, place, capacity):
    beside = LANES // capacity
    lanes = lane_index()
    tiles = [jnp.zeros((EDGE, LANES), f32)] * (packed_height(capacity) // EDGE)
    for a in range(EDGE):
        start = a % beside * capacity
        moved = pltpu.roll(
            section[a * EDGE : (a + 1) * EDGE], (start - place * capacity) % LANES, axis=1
        )
        inside = (lanes >= start) & (lanes < start + capacity)
        tiles[a // beside] = jnp.where(inside, moved, tiles[a // beside])
    return stacked(tiles)


def unpacked_section(own, blocks, order, capacity):
    beside = LANES // capacity
    lanes = lane_index()
    rows = [own[a * EDGE : (a + 1) * EDGE] for a in range(EDGE)]
    for place, block in zip(order, blocks):
        start = (place + 1) * capacity
        inside = (lanes >= start) & (lanes < start + capacity)
        for a in range(EDGE):
            tile = block[a // beside * EDGE : (a // beside + 1) * EDGE]
            moved = pltpu.roll(tile, (start - a % beside * capacity) % LANES, axis=1)
            rows[a] = jnp.where(inside, moved, rows[a])
    return stacked(rows)


def pack_pipes(pipe):
    half = PLANE // 2
    first = lane_index() < LANES // 2
    top, bottom = pipe[:half], pipe[half:]
    near = jnp.where(first, top, pltpu.roll(bottom, LANES // 2, axis=1))
    far = jnp.where(first, pltpu.roll(top, LANES // 2, axis=1), bottom)
    return near, far


def unpacked_pipes(near, far):
    first = lane_index() < LANES // 2
    top = jnp.where(first, near, pltpu.roll(far, LANES // 2, axis=1))
    bottom = jnp.where(first, pltpu.roll(near, LANES // 2, axis=1), far)
    return stacked([top, bottom])


def add_faces(cube_ref, grid_ref, codes_ref, hot_ref, values, start):
    slots = cube_ref.shape[1]
    last = EDGE - 1
    columns_used = slice(start, start + values.shape[1])
    codes = codes_ref[:, columns_used]
    odd = codes & 1 == 1
    second = codes & 2 == 2
    turned = codes >= 4
    turned_groups = []
    for group in range(values.shape[1] // LANES):
        span = slice(group * LANES, (group + 1) * LANES)
        base = group * PLANE
        whole = slice(base, base + PLANE)
        across = [pl.ds(base + b, EDGE, stride=EDGE) for b in range(EDGE)]
        rows = [values[a * EDGE : (a + 1) * EDGE, span] for a in range(EDGE)]
        rows = [jnp.where(odd[:, span], rows[last - a], rows[a]) for a in range(EDGE)]
        grid_ref[whole, :] = stacked(rows)
        columns = [grid_ref[place, :] for place in across]
        columns = [
            jnp.where(second[:, span], columns[last - b], columns[b]) for b in range(EDGE)
        ]
        grid_ref[whole, :] = stacked(columns)
        rows = [grid_ref[place, :] for place in across]
        rows = [jnp.where(turned[:, span], columns[a], rows[a]) for a in range(EDGE)]
        turned_groups.append(stacked(rows))
    grid = halves(jnp.concatenate(turned_groups, axis=1))
    extra = joined(
        lax.dot_general(
            grid, hot_ref[:, columns_used], (((1,), (1,)), ((), ())), preferred_element_type=f32
        )
    )
    parts = [extra[:, face * slots : (face + 1) * slots] for face in range(FACES)]
    cube_ref[0:PLANE, :] += parts[0]
    cube_ref[last * PLANE : EDGE * PLANE, :] += parts[1]
    for i in range(EDGE):
        piece = slice(i * EDGE, (i + 1) * EDGE)
        cube_ref[i * PLANE : i * PLANE + EDGE, :] += parts[2][piece]
        cube_ref[(i + 1) * PLANE - EDGE : (i + 1) * PLANE, :] += parts[3][piece]
    cube_ref[pl.ds(0, PLANE, stride=EDGE), :] += parts[4]
    cube_ref[pl.ds(last, PLANE, stride=EDGE), :] += parts[5]


def hat_pattern(side, slots):
    index = lax.broadcasted_iota(jnp.int32, (EDGE, slots), 0)
    pattern = jnp.full((EDGE, slots), number(HATS[side, 0]), f32)
    for k in range(1, EDGE):
        pattern = jnp.where(index == k, number(HATS[side, k]), pattern)
    return pattern


def hat_sum(side, members):
    total = None
    for weight, member in zip(HATS[side], members):
        if weight:
            term = member if weight == 1.0 else number(weight) * member
            total = term if total is None else total + term
    return total


def corner_sums(cube_ref):
    slots = cube_ref.shape[1]
    patterns = [hat_pattern(side, slots) for side in range(2)]
    rows = []
    for first in range(2):
        plane = hat_sum(first, [cube_ref[i * PLANE : (i + 1) * PLANE, :] for i in range(EDGE)])
        for second in range(2):
            line = hat_sum(second, [plane[j * EDGE : (j + 1) * EDGE] for j in range(EDGE)])
            for third in range(2):
                rows.append(jnp.sum(line * patterns[third], axis=0, keepdims=True))
    return rows


def hat_pair(pair, index):
    low, high = HATS[:, index]
    if high == 0.0:
        return pair[0]
    if low == 0.0:
        return pair[1]
    return number(low) * pair[0] + number(high) * pair[1]


def stacked(members):
    return jnp.concatenate(members, axis=0)


def lift_corners(rows, slots):
    patterns = [hat_pattern(side, slots) for side in range(2)]
    planes, slopes, rises = [], [], []
    for first in range(2):
        corners = [rows[4 * first + c] for c in range(4)]
        lines = [corners[2 * j] * patterns[0] + corners[2 * j + 1] * patterns[1] for j in range(2)]
        planes.append(stacked([hat_pair(lines, j) for j in range(EDGE)]))
        slopes.append(0.5 * (lines[1] - lines[0]))
        steps = [0.5 * (corners[2 * j + 1] - corners[2 * j]) for j in range(2)]
        rises.append(stacked([hat_pair(steps, j) for j in range(EDGE)]))
    field = [hat_pair(planes, i) for i in range(EDGE)]
    along_first = 0.5 * (planes[1] - planes[0])
    along_second = stacked([hat_pair(slopes, i) for i in range(EDGE)])
    along_third = stacked([hat_pair(rises, i) for i in range(EDGE)])
    return field, along_first, along_second, along_third


def coarse_terms(rows, vertex_ref, pieces):
    ids = corner_ids(vertex_ref)
    weights = jnp.concatenate(rows, axis=1)
    tall = max(pieces, EDGE)
    high = lax.broadcasted_iota(jnp.int32, (tall, ids.shape[1]), 0) == ids // LANES
    low = lax.broadcasted_iota(jnp.int32, (LANES, ids.shape[1]), 0) == ids % LANES
    total = joined(
        lax.dot_general(
            halves(jnp.where(high, weights, 0.0)),
            jnp.where(low, 1.0, 0.0).astype(bf16),
            (((1,), (1,)), ((), ())),
            preferred_element_type=f32,
        )
    )
    return total[:pieces]


def corner_ids(vertex_ref):
    return jnp.concatenate([vertex_ref[c : c + 1, :] for c in range(CORNERS)], axis=1)


def coarse_lookup(table, low_ref, high_ref, slots):
    taken = joined(jnp.dot(halves(table), low_ref[...], preferred_element_type=f32))
    taken = jnp.sum(taken * high_ref[...], axis=0, keepdims=True)
    return [taken[:, c * slots : (c + 1) * slots] for c in range(CORNERS)]


def smooth_kernel(
    live_ref,
    section_hbm,
    pipe_hbm,
    vectors_hbm,
    residual_hbm,
    values_hbm,
    vertex_hbm,
    terms_hbm,
    rmask_ref,
    smooth_ref,
    section_out,
    pipe_out,
    alive_ref,
    hot_ref,
    vertex_ref,
    corners_ref,
    section_ref,
    pipe_ref,
    vectors_ref,
    values_ref,
    spread_ref,
    first_ref,
    second_ref,
    terms_ref,
    arrivals,
):
    slots = rmask_ref.shape[1]
    targets = [
        (section_hbm, section_ref),
        (pipe_hbm, pipe_ref),
        (vectors_hbm, vectors_ref),
        (residual_hbm, rmask_ref),
        (values_hbm, values_ref),
        (vertex_hbm, vertex_ref),
    ]
    copies = begin(
        [(source, target, arrivals.at[n]) for n, (source, target) in enumerate(targets)]
    )
    alive = jnp.where(lane_index(1, slots) < live_ref[0], 1.0, 0.0)
    alive_ref[...] = alive
    for copy in copies[:2]:
        copy.wait()
    hot_ref[...] = one_hot(slot_columns(slots, section_ref, pipe_ref), FACES * slots)
    copies[2].wait()

    def spread(step, carry):
        block = vectors_ref[pl.ds(pl.multiple_of(step * EDGE, EDGE), EDGE), :]
        for row in range(EDGE):
            spread_ref[step * EDGE + row] = jnp.broadcast_to(block[row : row + 1], (EDGE, slots))
        return carry

    lax.fori_loop(0, 3 * EDGE, spread, 0)
    for copy in copies[3:]:
        copy.wait()
    rmask_ref[...] = rmask_ref[...] * alive
    rows = corner_sums(rmask_ref)
    corners_ref[...] = stacked(rows)
    terms = coarse_terms(rows, vertex_ref, terms_ref.shape[1])
    terms_ref[...] = jnp.broadcast_to(terms[None], terms_ref.shape)
    (departure,) = begin([(terms_ref, terms_hbm, arrivals.at[len(copies)])])

    def mix(direction, lines, turned):
        results = [[] for _ in lines]
        for a in range(EDGE):
            totals = [None] * len(lines)
            for b in range(EDGE):
                pair = a * EDGE + b if turned else b * EDGE + a
                weight = spread_ref[direction * PLANE + pair]
                for place, line in enumerate(lines):
                    term = weight * line[b]
                    totals[place] = term if b == 0 else totals[place] + term
            for result, total in zip(results, totals):
                result.append(total)
        return results

    def load(ref, places):
        return [[ref[place, :] for place in line] for line in places]

    def store(ref, places, lines):
        for line, members in zip(places, lines):
            for place, member in zip(line, members):
                ref[place, :] = member

    pair_of = range(2)

    def along_first(source_ref, target_ref, turned):
        def body(step, carry):
            at = [
                [
                    pl.ds(pl.multiple_of(i * PLANE + (2 * step + n) * EDGE, EDGE), EDGE)
                    for i in range(EDGE)
                ]
                for n in pair_of
            ]
            store(target_ref, at, mix(0, load(source_ref, at), turned))
            return carry

        lax.fori_loop(0, EDGE // 2, body, 0)

    along_first(rmask_ref, first_ref, False)

    def body(step, carry):
        bases = [pl.multiple_of((2 * step + n) * PLANE, PLANE) for n in pair_of]
        at = [[pl.ds(base + j * EDGE, EDGE) for j in range(EDGE)] for base in bases]
        across = [[pl.ds(base + k, EDGE, stride=EDGE) for k in range(EDGE)] for base in bases]
        store(second_ref, at, mix(1, load(first_ref, at), False))
        lines = mix(2, load(second_ref, across), False)
        for n in pair_of:
            shared = values_ref[pl.ds(2 * step + n, 1), :] + values_ref[EDGE : 2 * EDGE, :]
            lines[n] = [
                member / (shared + values_ref[2 * EDGE + c : 2 * EDGE + c + 1, :])
                for c, member in enumerate(lines[n])
            ]
        store(first_ref, across, mix(2, lines, True))
        store(second_ref, at, mix(1, load(first_ref, at), True))
        return carry

    lax.fori_loop(0, EDGE // 2, body, 0)
    along_first(second_ref, smooth_ref, True)
    pick_faces(smooth_ref, hot_ref, section_ref.shape[1], section_out, pipe_out)
    departure.wait()


def coarse_rows_kernel(inverse_ref, parts_ref, out_ref):
    total = added([parts_ref[device] for device in range(parts_ref.shape[0])])
    rows, vertices = inverse_ref.shape
    products = added(
        [
            inverse_ref[:, piece * LANES : (piece + 1) * LANES] * total[piece : piece + 1]
            for piece in range(vertices // LANES)
        ]
    )
    sums = jnp.broadcast_to(jnp.sum(products, axis=1, keepdims=True), (rows, LANES))
    own = lax.broadcasted_iota(jnp.int32, (rows, LANES), 0) == lane_index(rows)
    row = jnp.sum(jnp.where(own, sums, 0.0), axis=0, keepdims=True)
    out_ref[...] = jnp.broadcast_to(row, out_ref.shape)


def combine(matrix, values):
    half = EDGE // 2
    last = EDGE - 1
    sums = [values[b] + values[last - b] for b in range(half)]
    gaps = [values[b] - values[last - b] for b in range(half)]
    results = [None] * EDGE
    for a in range(half):
        even = sum(
            number(0.5 * (matrix[a, b] + matrix[a, last - b])) * sums[b] for b in range(half)
        )
        odd = sum(
            number(0.5 * (matrix[a, b] - matrix[a, last - b])) * gaps[b] for b in range(half)
        )
        results[a] = odd + even
        results[last - a] = odd - even
    return results


def face_kernel(
    blocks,
    capacity,
    own_rows,
    diagonal_hbm,
    cross_hbm,
    section_code_hbm,
    pipe_code_hbm,
    smooth_ref,
    rmask_ref,
    vertex_ref,
    alive_ref,
    hot_ref,
    *refs,
):
    block_refs, refs = refs[:blocks], refs[blocks:]
    part_ref, first_ref, second_ref, third_ref, diagonal_ref, cross_ref, *refs = refs
    sums_ref, low_ref, high_ref, codes_ref, grid_ref, *refs = refs
    section_code_ref, pipe_code_ref, arrivals = refs
    copies = begin(
        [
            (section_code_hbm, section_code_ref, arrivals.at[0]),
            (pipe_code_hbm, pipe_code_ref, arrivals.at[1]),
            (diagonal_hbm, diagonal_ref, arrivals.at[2]),
            (cross_hbm, cross_ref, arrivals.at[3]),
        ]
    )
    rmask = rmask_ref[...]
    sums_ref[EDGE : 2 * EDGE, :] = fold(rmask * rmask)
    ids = corner_ids(vertex_ref)
    low = lax.broadcasted_iota(jnp.int32, low_ref.shape, 0) == ids % own_rows
    high = lax.broadcasted_iota(jnp.int32, high_ref.shape, 0) == ids // own_rows
    low_ref[...] = jnp.where(low, 1.0, 0.0).astype(bf16)
    high_ref[...] = jnp.where(high, 1.0, 0.0)
    part_ref[:POINTS, :] = smooth_ref[:POINTS, :]
    for copy in copies[:2]:
        copy.wait()
    codes_ref[...] = slot_codes(section_code_ref, pipe_code_ref)
    own_ref, far_ref, near_ref, *arrived = block_refs
    order = arrival_order(len(arrived))
    section = section_columns(capacity, [own_ref, *arrived], order)
    values = jnp.concatenate([section, pipe_columns(near_ref, far_ref)], axis=1)
    add_faces(part_ref, grid_ref, codes_ref, hot_ref, values, 0)
    alive = alive_ref[...]
    part_ref[:POINTS, :] = alive * part_ref[:POINTS, :]

    def gradient(step, carry):
        base = pl.multiple_of(step * PLANE, PLANE)
        row = pl.multiple_of(step * EDGE, EDGE)
        for target_ref, places in (
            (first_ref, [pl.ds(i * PLANE + row, EDGE) for i in range(EDGE)]),
            (second_ref, [pl.ds(base + j * EDGE, EDGE) for j in range(EDGE)]),
            (third_ref, [pl.ds(base + k, EDGE, stride=EDGE) for k in range(EDGE)]),
        ):
            values = combine(DERIVATIVE, [part_ref[place, :] for place in places])
            for place, member in zip(places, values):
                target_ref[place, :] = member
        return carry

    lax.fori_loop(0, EDGE, gradient, 0)
    sums_ref[0:EDGE, :] = fold(rmask * part_ref[:POINTS, :])
    for copy in copies[2:]:
        copy.wait()


def operator_kernel(
    capacity,
    own_rows,
    part_ref,
    grad_first_ref,
    grad_second_ref,
    grad_third_ref,
    diagonal_ref,
    cross_ref,
    known_ref,
    low_ref,
    high_ref,
    corners_ref,
    alive_ref,
    hot_ref,
    coarse_ref,
    direction_ref,
    applied_ref,
    section_out,
    sums_out,
    near_out,
    far_out,
    *refs,
):
    *packed_outs, first_ref, third_ref, slope_ref, rise_ref, pipe_ref = refs
    slots = direction_ref.shape[1]
    backward = DERIVATIVE.T
    alive = alive_ref[...]
    rows = coarse_lookup(coarse_ref[:, :own_rows], low_ref, high_ref, slots)
    rows = [alive * row for row in rows]
    field, along_first, along_second, along_third = lift_corners(rows, slots)
    for i, plane in enumerate(field):
        whole = slice(i * PLANE, (i + 1) * PLANE)
        direction_ref[whole, :] = part_ref[whole, :] + plane
    slope_ref[...] = along_second
    rise_ref[...] = along_third

    def fluxes(step, curvature):
        base = pl.multiple_of(step * PLANE, PLANE)
        whole = pl.ds(base, PLANE)
        line = pl.ds(pl.multiple_of(step * EDGE, EDGE), EDGE)
        field = direction_ref[whole, :]
        slope = slope_ref[line, :]
        rise = rise_ref[line, :]
        grad_first = grad_first_ref[whole, :] + along_first
        grad_second = grad_second_ref[whole, :] + stacked([slope] * EDGE)
        grad_third = grad_third_ref[whole, :] + stacked(
            [jnp.broadcast_to(rise[j : j + 1], (EDGE, slots)) for j in range(EDGE)]
        )
        diagonal = [diagonal_ref[d, whole, :].astype(f32) for d in range(3)]
        cross = [cross_ref[d, whole, :].astype(f32) for d in range(3)]
        flux_first = diagonal[0] * grad_first + cross[0] * grad_second + cross[1] * grad_third
        flux_second = cross[0] * grad_first + diagonal[1] * grad_second + cross[2] * grad_third
        flux_third = cross[1] * grad_first + cross[2] * grad_second + diagonal[2] * grad_third
        energy = (
            grad_first * flux_first
            + grad_second * flux_second
            + grad_third * flux_third
            + field * field
        )
        first_ref[whole, :] = flux_first
        third_ref[whole, :] = flux_third
        rows = [flux_second[j * EDGE : (j + 1) * EDGE] for j in range(EDGE)]
        applied_ref[whole, :] = field + stacked(combine(backward, rows))
        return curvature + fold(energy)

    empty = jnp.zeros((EDGE, slots), f32)
    curvature = lax.fori_loop(0, EDGE, fluxes, empty, unroll=True)
    precond = known_ref[0:EDGE, :] + corners_ref[...] * stacked(rows)
    sums = [precond, curvature, known_ref[EDGE : 2 * EDGE, :]]

    def divergence(step, carry):
        base = pl.multiple_of(step * PLANE, PLANE)
        row = pl.multiple_of(step * EDGE, EDGE)
        for source_ref, places in (
            (first_ref, [pl.ds(i * PLANE + row, EDGE) for i in range(EDGE)]),
            (third_ref, [pl.ds(base + k, EDGE, stride=EDGE) for k in range(EDGE)]),
        ):
            values = combine(backward, [source_ref[place, :] for place in places])
            for place, member in zip(places, values):
                applied_ref[place, :] += member
        return carry

    lax.fori_loop(0, EDGE, divergence, 0, unroll=True)
    pick_faces(applied_ref, hot_ref, capacity, section_out, pipe_ref)
    section = section_out[...]
    for place, packed_out in enumerate(packed_outs):
        packed_out[...] = pack_section(section, place + 1, capacity)
    near_out[...], far_out[...] = pack_pipes(pipe_ref[...])
    row = lane_row([total_of(member) for member in sums])
    sums_out[...] = jnp.broadcast_to(row, sums_out.shape)


def pipe_kernel(applied_ref, codes_ref, hot_ref, near_ref, far_ref, image_ref, grid_ref):
    image_ref[:POINTS, :] = applied_ref[:POINTS, :]
    values = unpacked_pipes(near_ref[...], far_ref[...])
    add_faces(
        image_ref, grid_ref, codes_ref, hot_ref, values, codes_ref.shape[1] - values.shape[1]
    )


def image_kernel(capacity, rmask_ref, partial_ref, codes_ref, hot_ref, sums_ref, *refs):
    *block_refs, image_ref, sums_out, grid_ref = refs
    image_ref[:POINTS, :] = partial_ref[:POINTS, :]
    own_ref, *arrived = block_refs
    values = unpacked_section(
        own_ref[...],
        [block_ref[...] for block_ref in arrived],
        reversed(arrival_order(len(arrived))),
        capacity,
    )
    add_faces(image_ref, grid_ref, codes_ref, hot_ref, values, 0)
    image = image_ref[:POINTS, :]
    rmask = rmask_ref[...]
    square = total_of(image * image)
    product = total_of(rmask * image)
    near = jnp.where(square > 0.0, product / jnp.where(square > 0.0, square, 1.0), 0.0)
    rest = rmask - near * image
    row = lane_row(
        [sums_ref[0:1, n : n + 1] for n in range(3)]
        + [total_of(rest * rest), total_of(rest * image), square, near]
    )
    sums_out[...] = jnp.broadcast_to(row, sums_out.shape)


def update_kernel(
    rmask_ref,
    solution_ref,
    direction_ref,
    image_ref,
    alive_ref,
    sums_ref,
    solution_out,
    residual_out,
    ratio_out,
):
    alive = alive_ref[...]
    sums = sums_ref[...]
    whole = jnp.sum(sums, axis=0, keepdims=True)
    step_length = whole[:, 0:1] / whole[:, 1:2]
    solution_out[...] = alive * (solution_ref[...] + step_length * direction_ref[...])
    residual_out[...] = rmask_ref[...] - step_length * image_ref[:POINTS, :]
    gap = step_length - sums[:, 6:7]
    fresh = sums[:, 3:4] - 2.0 * gap * sums[:, 4:5] + gap * gap * sums[:, 5:6]
    ratio_out[0] = jnp.sum(fresh) / jnp.sum(whole[:, 2:3])


def kernel_call(body, outputs, scratch=(), remote=0, copies=0, leaving=()):
    def call(*operands):
        memory, given = [], []
        for place, operand in enumerate(operands):
            if operand.ndim == 1:
                memory.append(pltpu.SMEM)
            elif place < remote:
                memory.append(pltpu.HBM)
                operand = pltpu.with_memory_space_constraint(operand, pltpu.HBM)
            else:
                memory.append(pltpu.VMEM)
            given.append(operand)
        shapes, spaces = [], []
        for place, output in enumerate(outputs):
            shape, kind = output if isinstance(output[0], tuple) else (output, f32)
            shapes.append(jax.ShapeDtypeStruct(shape, kind))
            if place in leaving:
                spaces.append(pl.ANY)
            else:
                spaces.append(pltpu.SMEM if len(shape) == 1 else pltpu.VMEM)
        return pl.pallas_call(
            body,
            out_shape=tuple(shapes),
            in_specs=[pl.BlockSpec(memory_space=space) for space in memory],
            out_specs=tuple(pl.BlockSpec(memory_space=space) for space in spaces),
            scratch_shapes=[pltpu.VMEM(shape, kind) for shape, kind in scratch]
            + ([pltpu.SemaphoreType.DMA((copies,))] if copies else []),
            compiler_params=pltpu.CompilerParams(vmem_limit_bytes=40 << 20),
        )(*given)

    return call


def held(array):
    return (array.shape, array.dtype)


def exchange(values):
    return lax.all_to_all(values, AXES, split_axis=0, concat_axis=0, tiled=True)


def swap(values, axis, table):
    return lax.ppermute(values, axis, [(int(i), int(table[i])) for i in range(len(table))])


def arrival_order(sections):
    return [0, *range(2, sections), 1]


def swap_faces(section, pipe):
    tables = section_pairings(lax.axis_size("gy"))
    near, far = pairings(lax.axis_size("gx"))
    near_pipe = swap(pipe, "gx", near)
    arrived = [swap(section, "gy", tables[place]) for place in arrival_order(len(tables))]
    return [section, near_pipe, *arrived, swap(pipe, "gx", far)]


def on_device(
    solution,
    residual,
    metric_diag,
    metric_cross,
    fdm_vectors,
    fdm_values,
    vertex_ids,
    coarse_inverse,
    elem_live,
    section_face,
    section_code,
    pipe_face,
    pipe_code,
):
    field = residual.shape
    slots = field[1]
    own_rows, vertices = coarse_inverse.shape
    devices = lax.axis_size(AXES)
    peers, capacity = section_face.shape[1:]
    vectors = fdm_vectors.reshape(-1, slots)
    values = fdm_values.reshape(-1, slots)
    lists = [section_face[0], pipe_face[0]]
    codes = [section_code[0], pipe_code[0]]
    blocks = len(section_pairings(peers)) + 3
    section_width = -(-(blocks - 2) * capacity // LANES) * LANES
    pipe_width = 2 * pipe_face.shape[2]
    width = section_width + pipe_width
    sends = [(PLANE, section_width), (PLANE, pipe_width)]
    grid = ((PLANE * width // LANES + EDGE, LANES), f32)
    tall = (TALL, slots)
    pieces = vertices // LANES
    message = (devices, LANES)

    direct = devices * vertices * 4 <= DIRECT_BYTES
    copies = devices if direct else 1
    given = [elem_live, *lists, vectors, residual, values, vertex_ids]
    terms = (copies, pieces, LANES)
    hot = ((FACES * slots, width), bf16)
    parts, rmask, smooth, section_sent, pipe_sent, alive, hot, vertex_ids, corners = kernel_call(
        smooth_kernel,
        [
            terms,
            field,
            tall,
            *sends,
            (1, slots),
            hot,
            held(vertex_ids),
            (CORNERS, slots),
        ],
        [held(member) for member in [*lists, vectors, values]]
        + [((3 * PLANE, EDGE, slots), f32), (tall, f32), (tall, f32), (terms, f32)],
        remote=len(given),
        copies=len(given),
        leaving=(0,),
    )(*given)
    parts = exchange(parts) if direct else lax.psum(parts, AXES)
    own, near_pipe, *arrived, far_pipe = swap_faces(section_sent, pipe_sent)
    faces = [own, far_pipe, near_pipe, *arrived]
    (coarse,) = kernel_call(coarse_rows_kernel, [message])(coarse_inverse, parts)
    coarse = exchange(coarse)
    corner_count = CORNERS * slots
    known = kernel_call(
        functools.partial(face_kernel, blocks, capacity, own_rows),
        [
            tall,
            tall,
            tall,
            tall,
            held(metric_diag),
            held(metric_cross),
            (2 * EDGE, slots),
            ((own_rows, corner_count), bf16),
            (devices, corner_count),
            ((EDGE, width), jnp.int32),
        ],
        [grid, *(held(member) for member in codes)],
        remote=4,
        copies=4,
    )(metric_diag, metric_cross, *codes, smooth, rmask, vertex_ids, alive, hot, *faces)
    *known, codes = known
    small = (packed_height(capacity), LANES)
    side = (PLANE // 2, LANES)
    direction, applied, own, sums, near_pipe, far_pipe, *packed = kernel_call(
        functools.partial(operator_kernel, capacity, own_rows),
        [field, tall, sends[0], (1, LANES), side, side] + [small] * (blocks - 3),
        [(tall, f32)] * 2 + [((PLANE, slots), f32)] * 2 + [(sends[1], f32)],
    )(*known, corners, alive, hot, coarse)
    tables = section_pairings(peers)
    near, far = pairings(lax.axis_size("gx"))
    order = reversed(arrival_order(len(tables)))
    arrived = [swap(packed[place], "gy", tables[place]) for place in order]
    near_pipe, far_pipe = swap(near_pipe, "gx", near), swap(far_pipe, "gx", far)
    (partial,) = kernel_call(pipe_kernel, [tall], [grid])(
        applied, codes, hot, near_pipe, far_pipe
    )
    image, sums = kernel_call(
        functools.partial(image_kernel, capacity), [tall, message], [grid]
    )(rmask, partial, codes, hot, sums, own, *arrived)
    solution_out, residual_out, norm_ratio = kernel_call(update_kernel, [field, field, (1,)])(
        rmask, solution, direction, image, alive, exchange(sums)
    )
    return (solution_out, residual_out, norm_ratio)


def solution(mesh):
    placed = (
        P(None, AXES),
        P(None, AXES),
        P(None, None, AXES),
        P(None, None, AXES),
        P(None, None, None, AXES),
        P(None, None, AXES),
        P(None, AXES),
        P(AXES, None),
        P(AXES),
        P(AXES, None, None),
        P(AXES, None, None),
        P(AXES, None, None),
        P(AXES, None, None),
    )
    return jax.shard_map(
        on_device,
        mesh=mesh,
        in_specs=placed,
        out_specs=(P(None, AXES), P(None, AXES), P()),
        check_vma=False,
    )
```

time: 310 us -> 48.8 us (0.16)
  blocking collectives: 160 us -> 9.82 us
  local copies, waits for them, and re-layouts: 89.9 us -> 0.01 us
  other arithmetic: 30.2 us -> 0 us
  waiting for transfers between devices: 0.02 us -> 8.06 us
  Pallas kernels: 0 us -> 7.95 us
  between operations: 9.19 us -> 1.41 us
  starting transfers between devices: 16.8 us -> 21.3 us
    psum x3 -> x0, blocking collectives: 120 us -> none  [the longest x1 41.8 us: on_device(): fresh_norm = lax.psum(jnp.sum(residual_out * residual_out), ('gx', 'gy'))]
    unnamed x1 -> x0, blocking collectives: 40.6 us -> none
    mul x104 -> x0, local copies, waits for them, and re-layouts: 25.8 us -> none  [the longest x78 20.9 us: contract(): total = total + matrices[index][:, None, None, :] * moved[index][None]]
    unnamed x304 -> x4, local copies, waits for them, and re-layouts: 16.6 us -> 0.01 us
    another operation x19 -> x0, local copies, waits for them, and re-layouts: 16.1 us -> none
    gather x5 -> x0, local copies, waits for them, and re-layouts: 13.7 us -> none  [the longest x1 6.86 us: on_device(): coarse_sol[vertex_ids]]
    scatter-add x11 -> x0, other arithmetic: 12.8 us -> none  [the longest x1 7.74 us: on_device(): jax.ops.segment_sum(corners.reshape(-1), vertex_ids.reshape(-1), num_segm...]
    all_to_all x0 -> x1, blocking collectives: none -> 9.82 us  [exchange(): return lax.all_to_all(values, AXES, split_axis=0, concat_axis=0, tiled=True)]
  transfers between devices with their start and end apart: 6 -> 12, of which waited for: 0 -> 4; matrix products, arithmetic and copies ran while one was open for 19% -> 0% of each run, Pallas kernels for 0% -> 5%
where the time goes in v1:
time: 48.8 us; the launch traced here: 48.5 us
  starting transfers between devices  21.3 us (44%)
  blocking collectives  9.82 us (20%)
  waiting for transfers between devices  8.06 us (17%)
  Pallas kernels  7.95 us (16%)
  between operations  1.41 us (3%)
    ppermute x10, starting transfers between devices, swap(): lax.ppermute(values, axis, [(int(i), int(table[i])) for i in range(len(ta...  11.4 us
    all_to_all x2, starting transfers between devices, exchange(): return lax.all_to_all(values, AXES, split_axis=0, concat_axis=0, tiled=True)  9.85 us
    all_to_all x1, blocking collectives, exchange(): return lax.all_to_all(values, AXES, split_axis=0, concat_axis=0, tiled=True)  9.82 us
    pallas_call x7, Pallas kernels, call(): pl.pallas_call(body, out_shape=tuple(shapes), in_specs=[pl.BlockSpec(memo...  7.95 us
    all_to_all x2, waiting for transfers between devices, exchange(): return lax.all_to_all(values, AXES, split_axis=0, concat_axis=0, tiled=True)  6.13 us
    ppermute x10, waiting for transfers between devices, swap(): lax.ppermute(values, axis, [(int(i), int(table[i])) for i in range(len(ta...  1.94 us
  transfers between devices with their start and end apart: 12, of which 4 were waited for; matrix products, arithmetic and copies ran while one was open for 0% of the time, Pallas kernels for 5%

profile of v1, /device:TPU:0, one launch (start us, length us, event | category | flops | bytes accessed | tf_op | source)
XLA Modules:
  0.0 48.5 jit_solution(11222644146515271445)
XLA Ops:
  1.3 2.8 %shard_map.148 = (f32[32,4,128]{2,1,0:T(4,128)}, f32[512,128]{1,0:T(8,128)S(1)}, f32[520,128]{1,0:T(8,128)S(1)}, f32[64,128]{1,0:T(8,128)S(1)}, f32[64,128]{1,0:...) custom-call(s32[1]{0:T(128)S(6)} %copy.18.live_ref, ...), custom_call_target="tpu_custom_call" | custom-call | tf_op jit(solution)/shard_map/pallas_call | solution.py:774
  4.1 0.0 copy-start.1
  4.1 7.3 %all-to-all-start = ((f32[32,4,128]{2,1,0:T(4,128)}), f32[32,4,128]{2,1,0:T(4,128)S(1)}, u32[]{:S(2)}, u32[]{:S(2)}) async-start(f32[32,4,128]{2,1,0:T(4,128)} %get-tuple-element.50), calls=%async_computation | async-start | bytes 131072 | tf_op jit(solution)/shard_map/all_to_all | solution.py:792
  11.4 0.3 collective-permute-start.1
  11.7 3.5 %collective-permute-start = (f32[64,128]{1,0:T(8,128)S(1)}, f32[64,128]{1,0:T(8,128)S(1)}, u32[]{:S(2)}, u32[]{:S(2)}) collective-permute-start(f32[64,128]{1,0:T(8,128)S(1)} %get-tuple-element.39), channel_id=1, source_target_pairs={{0,28},{4,8},{8,4},{12,16},{16,12},{20,24},{24,20},{28,0},{1,29},{... | collective-permute-start | bytes 98312 | tf_op jit(solution)/shard_map/ppermute | solution.py:796
  15.2 2.4 %collective-permute-start.4 = (f32[64,128]{1,0:T(8,128)S(1)}, f32[64,128]{1,0:T(8,128)S(1)}, u32[]{:S(2)}, u32[]{:S(2)}) collective-permute-start(f32[64,128]{1,0:T(8,128)S(1)} %get-tuple-element.38.refs_0_), channel_id=1, source_target_pairs={{0,3},{1,2},{2,1},{3,0},{4,7},{5,6},{6,5},{7,4},{8,11},{9,10},{10,... | collective-permute-start | bytes 98312 | tf_op jit(solution)/shard_map/ppermute | solution.py:796
  17.6 0.5 %collective-permute-start.3 = (f32[64,128]{1,0:T(8,128)S(1)}, f32[64,128]{1,0:T(8,128)S(1)}, u32[]{:S(2)}, u32[]{:S(2)}) collective-permute-start(f32[64,128]{1,0:T(8,128)S(1)} %get-tuple-element.38.refs_0_), channel_id=1, source_target_pairs={{0,2},{1,3},{2,0},{3,1},{4,6},{5,7},{6,4},{7,5},{8,10},{9,11},{10,... | collective-permute-start | bytes 98312 | tf_op jit(solution)/shard_map/ppermute | solution.py:796
  18.1 0.5 %collective-permute-start.2 = (f32[64,128]{1,0:T(8,128)S(1)}, f32[64,128]{1,0:T(8,128)S(1)}, u32[]{:S(2)}, u32[]{:S(2)}) collective-permute-start(f32[64,128]{1,0:T(8,128)S(1)} %get-tuple-element.38.refs_0_), channel_id=1, source_target_pairs={{0,1},{1,0},{2,3},{3,2},{4,5},{5,4},{6,7},{7,6},{8,9},{9,8},{10,11... | collective-permute-start | bytes 98312 | tf_op jit(solution)/shard_map/ppermute | solution.py:796
  18.7 0.6 %all-to-all-done.parts_ref = f32[32,4,128]{2,1,0:T(4,128)S(1)} async-done(((f32[32,4,128]{2,1,0:T(4,128)}), f32[32,4,128]{2,1,0:T(4,128)S(1)}, u32[]{:S(2)}, u32[]{:S(2)}) %all-to-all-start) | async-done | bytes 65568 | tf_op jit(solution)/shard_map/all_to_all | solution.py:792
  19.2 0.0 copy-done.1
  19.2 0.7 %shard_map.150 = f32[32,128]{1,0:T(8,128)} custom-call(f32[16,512]{1,0:T(8,128)S(1)} %copy-done.1, f32[32,4,128]{2,1,0:T(4,128)S(1)} %all-to-all-done.parts_ref), custom_call_target="tpu_custom_call" | custom-call | tf_op jit(solution)/shard_map/pallas_call | solution.py:774
  20.0 2.5 %all-to-all-start.1 = ((f32[32,1,128]{2,1,0:T(1,128)}), f32[32,1,128]{2,1,0:T(1,128)S(1)}, u32[]{:S(2)}, u32[]{:S(2)}) async-start(f32[32,1,128]{2,1,0:T(1,128)} %bitcast.7), calls=%async_computation.1 | async-start | bytes 32768 | tf_op jit(solution)/shard_map/all_to_all | solution.py:792
  22.5 0.0 collective-permute-done.1.refs_2_
  22.5 0.0 collective-permute-done.refs_1_
  22.5 0.0 collective-permute-done.4.refs_5_
  22.5 0.0 collective-permute-done.3.refs_4_
  22.5 0.0 collective-permute-done.2.refs_3_
  22.6 1.5 %shard_map.149 = (f32[520,128]{1,0:T(8,128)S(1)}, f32[520,128]{1,0:T(8,128)S(1)}, f32[520,128]{1,0:T(8,128)S(1)}, f32[520,128]{1,0:T(8,128)S(1)}, bf16[3,512,128...) custom-call(bf16[3,512,128]{2,1,0:T(8,128)(2,1)} %diagonal_hbm.1, ...), custom_call_target="tpu_custom_call" | custom-call | tf_op jit(solution)/shard_map/pallas_call | solution.py:774
  24.0 5.6 %all-to-all-done.1 = f32[32,1,128]{2,1,0:T(1,128)S(1)} async-done(((f32[32,1,128]{2,1,0:T(1,128)}), f32[32,1,128]{2,1,0:T(1,128)S(1)}, u32[]{:S(2)}, u32[]{:S(2)}) %all-to-all-start.1) | async-done | bytes 16416 | tf_op jit(solution)/shard_map/all_to_all | solution.py:792
  29.6 1.2 %shard_map.151 = (f32[512,128]{1,0:T(8,128)S(1)}, f32[520,128]{1,0:T(8,128)S(1)}, f32[64,128]{1,0:T(8,128)S(1)}, f32[1,128]{1,0:T(1,128)S(1)}, f32[32,128]{1,0:T...) custom-call(f32[520,128]{1,0:T(8,128)S(1)} %get-tuple-element.40.par, ...), custom_call_target="tpu_custom_call" | custom-call | tf_op jit(solution)/shard_map/pallas_call | solution.py:774
  30.8 0.1 collective-permute-start.5
  30.8 0.6 %collective-permute-start.6 = (f32[32,128]{1,0:T(8,128)S(1)}, f32[32,128]{1,0:T(8,128)S(1)}, u32[]{:S(2)}, u32[]{:S(2)}) collective-permute-start(f32[32,128]{1,0:T(8,128)S(1)} %get-tuple-element.55), channel_id=1, source_target_pairs={{0,28},{4,8},{8,4},{12,16},{16,12},{20,24},{24,20},{28,0},{1,29},{... | collective-permute-start | bytes 49160 | tf_op jit(solution)/shard_map/ppermute | solution.py:796
  31.4 0.6 %collective-permute-start.7 = (f32[16,128]{1,0:T(8,128)S(1)}, f32[16,128]{1,0:T(8,128)S(1)}, u32[]{:S(2)}, u32[]{:S(2)}) collective-permute-start(f32[16,128]{1,0:T(8,128)S(1)} %get-tuple-element.58), channel_id=1, source_target_pairs={{0,3},{1,2},{2,1},{3,0},{4,7},{5,6},{6,5},{7,4},{8,11},{9,10},{10,... | collective-permute-start | bytes 24584 | tf_op jit(solution)/shard_map/ppermute | solution.py:796
  32.0 1.5 %collective-permute-start.8 = (f32[16,128]{1,0:T(8,128)S(1)}, f32[16,128]{1,0:T(8,128)S(1)}, u32[]{:S(2)}, u32[]{:S(2)}) collective-permute-start(f32[16,128]{1,0:T(8,128)S(1)} %get-tuple-element.59), channel_id=1, source_target_pairs={{0,2},{1,3},{2,0},{3,1},{4,6},{5,7},{6,4},{7,5},{8,10},{9,11},{10,... | collective-permute-start | bytes 24584 | tf_op jit(solution)/shard_map/ppermute | solution.py:796
  33.5 1.4 %collective-permute-start.9 = (f32[16,128]{1,0:T(8,128)S(1)}, f32[16,128]{1,0:T(8,128)S(1)}, u32[]{:S(2)}, u32[]{:S(2)}) collective-permute-start(f32[16,128]{1,0:T(8,128)S(1)} %get-tuple-element.60), channel_id=1, source_target_pairs={{0,1},{1,0},{2,3},{3,2},{4,5},{5,4},{6,7},{7,6},{8,9},{9,8},{10,11... | collective-permute-start | bytes 24584 | tf_op jit(solution)/shard_map/ppermute | solution.py:796
  34.9 0.0 collective-permute-done.5.near_ref
  34.9 1.0 %collective-permute-done.6.far_ref = f32[32,128]{1,0:T(8,128)S(1)} collective-permute-done((f32[32,128]{1,0:T(8,128)S(1)}, f32[32,128]{1,0:T(8,128)S(1)}, u32[]{:S(2)}, u32[]{:S(2)}) %collective-permute-start.6) | collective-permute-done | bytes 16416 | tf_op jit(solution)/shard_map/ppermute | solution.py:796
  35.9 0.3 shard_map.152.partial_ref
  36.2 0.0 collective-permute-done.7.refs_1_
  36.2 0.0 collective-permute-done.8.refs_2_
  36.2 1.0 %collective-permute-done.9.refs_3_ = f32[16,128]{1,0:T(8,128)S(1)} collective-permute-done((f32[16,128]{1,0:T(8,128)S(1)}, f32[16,128]{1,0:T(8,128)S(1)}, u32[]{:S(2)}, u32[]{:S(2)}) %collective-permute-start.9) | collective-permute-done | bytes 8224 | tf_op jit(solution)/shard_map/ppermute | solution.py:796
  37.1 0.0 copy-start
  37.1 0.6 %shard_map.153 = (f32[520,128]{1,0:T(8,128)S(1)}, f32[32,128]{1,0:T(8,128)S(1)}) custom-call(f32[512,128]{1,0:T(8,128)S(1)} %get-tuple-element.33.rmask_ref, f32[520,128]{1,0:T(8,128)S(1)} %shard_map.152.partial_ref, s32[8,256]{1,0:T(8,128)S(1)} %get-tuple-element.53.codes_ref, bf16[768,256]{1,0:T(8,128)(2,1)S(1)} %get-tuple-element.37.hot_ref, ...), custom_call_target="tpu_custom_call" | custom-call | tf_op jit(solution)/shard_map/pallas_call | solution.py:774
  37.7 9.8 %all_to_all.27 = f32[32,1,128]{2,1,0:T(1,128)S(1)} all-to-all(f32[32,1,128]{2,1,0:T(1,128)S(1)} %bitcast.16), channel_id=1, replica_groups=mesh['gx'=8,'gy'=4] {'gx','gy'}, dimensions={0} | all-to-all | bytes 32768 | tf_op jit(solution)/shard_map/all_to_all | solution.py:792
  47.5 0.0 copy-done
  47.5 1.0 %shard_map.154 = (f32[512,128]{1,0:T(8,128)}, f32[512,128]{1,0:T(8,128)}, f32[1]{0:T(128)}) custom-call(f32[512,128]{1,0:T(8,128)S(1)} %get-tuple-element.33.rmask_ref, f32[512,128]{1,0:T(8,128)S(1)} %copy-done, f32[512,128]{1,0:T(8,128)S(1)} %get-tuple-element.51.direction_ref, f32[520,128]{1,0:T(8,128)S(1)} %get-tuple-element.61.image_ref, ...), custom_call_target="tpu_custom_call" | custom-call | tf_op jit(solution)/shard_map/pallas_call | solution.py:774
Async XLA Ops:
  4.1 15.2 %copy-start.1 = (f32[16,512]{1,0:T(8,128)S(1)}, f32[16,512]{1,0:T(8,128)}, u32[]{:S(2)}) copy-start(f32[16,512]{1,0:T(8,128)} %inverse_ref.1) | copy-start | bytes 98308
  4.1 15.2 %all-to-all-start = ((f32[32,4,128]{2,1,0:T(4,128)}), f32[32,4,128]{2,1,0:T(4,128)S(1)}, u32[]{:S(2)}, u32[]{:S(2)}) async-start(f32[32,4,128]{2,1,0:T(4,128)} %get-tuple-element.50), calls=%async_computation | async-start | bytes 131072 | tf_op jit(solution)/shard_map/all_to_all | solution.py:792
  11.4 11.1 %collective-permute-start.1 = (f32[64,128]{1,0:T(8,128)S(1)}, f32[64,128]{1,0:T(8,128)S(1)}, u32[]{:S(2)}, u32[]{:S(2)}) collective-permute-start(f32[64,128]{1,0:T(8,128)S(1)} %get-tuple-element.39), channel_id=1, source_target_pairs={{0,4},{4,0},{8,12},{12,8},{16,20},{20,16},{24,28},{28,24},{1,5},{5... | collective-permute-start | bytes 98312 | tf_op jit(solution)/shard_map/ppermute | solution.py:796
  11.7 10.8 %collective-permute-start = (f32[64,128]{1,0:T(8,128)S(1)}, f32[64,128]{1,0:T(8,128)S(1)}, u32[]{:S(2)}, u32[]{:S(2)}) collective-permute-start(f32[64,128]{1,0:T(8,128)S(1)} %get-tuple-element.39), channel_id=1, source_target_pairs={{0,28},{4,8},{8,4},{12,16},{16,12},{20,24},{24,20},{28,0},{1,29},{... | collective-permute-start | bytes 98312 | tf_op jit(solution)/shard_map/ppermute | solution.py:796
  15.2 7.3 %collective-permute-start.4 = (f32[64,128]{1,0:T(8,128)S(1)}, f32[64,128]{1,0:T(8,128)S(1)}, u32[]{:S(2)}, u32[]{:S(2)}) collective-permute-start(f32[64,128]{1,0:T(8,128)S(1)} %get-tuple-element.38.refs_0_), channel_id=1, source_target_pairs={{0,3},{1,2},{2,1},{3,0},{4,7},{5,6},{6,5},{7,4},{8,11},{9,10},{10,... | collective-permute-start | bytes 98312 | tf_op jit(solution)/shard_map/ppermute | solution.py:796
  17.6 4.9 %collective-permute-start.3 = (f32[64,128]{1,0:T(8,128)S(1)}, f32[64,128]{1,0:T(8,128)S(1)}, u32[]{:S(2)}, u32[]{:S(2)}) collective-permute-start(f32[64,128]{1,0:T(8,128)S(1)} %get-tuple-element.38.refs_0_), channel_id=1, source_target_pairs={{0,2},{1,3},{2,0},{3,1},{4,6},{5,7},{6,4},{7,5},{8,10},{9,11},{10,... | collective-permute-start | bytes 98312 | tf_op jit(solution)/shard_map/ppermute | solution.py:796
  18.1 4.4 %collective-permute-start.2 = (f32[64,128]{1,0:T(8,128)S(1)}, f32[64,128]{1,0:T(8,128)S(1)}, u32[]{:S(2)}, u32[]{:S(2)}) collective-permute-start(f32[64,128]{1,0:T(8,128)S(1)} %get-tuple-element.38.refs_0_), channel_id=1, source_target_pairs={{0,1},{1,0},{2,3},{3,2},{4,5},{5,4},{6,7},{7,6},{8,9},{9,8},{10,11... | collective-permute-start | bytes 98312 | tf_op jit(solution)/shard_map/ppermute | solution.py:796
  20.0 9.6 %all-to-all-start.1 = ((f32[32,1,128]{2,1,0:T(1,128)}), f32[32,1,128]{2,1,0:T(1,128)S(1)}, u32[]{:S(2)}, u32[]{:S(2)}) async-start(f32[32,1,128]{2,1,0:T(1,128)} %bitcast.7), calls=%async_computation.1 | async-start | bytes 32768 | tf_op jit(solution)/shard_map/all_to_all | solution.py:792
  30.8 4.1 %collective-permute-start.5 = (f32[32,128]{1,0:T(8,128)S(1)}, f32[32,128]{1,0:T(8,128)S(1)}, u32[]{:S(2)}, u32[]{:S(2)}) collective-permute-start(f32[32,128]{1,0:T(8,128)S(1)} %get-tuple-element.54), channel_id=1, source_target_pairs={{0,4},{4,0},{8,12},{12,8},{16,20},{20,16},{24,28},{28,24},{1,5},{5... | collective-permute-start | bytes 49160 | tf_op jit(solution)/shard_map/ppermute | solution.py:796
  30.8 5.0 %collective-permute-start.6 = (f32[32,128]{1,0:T(8,128)S(1)}, f32[32,128]{1,0:T(8,128)S(1)}, u32[]{:S(2)}, u32[]{:S(2)}) collective-permute-start(f32[32,128]{1,0:T(8,128)S(1)} %get-tuple-element.55), channel_id=1, source_target_pairs={{0,28},{4,8},{8,4},{12,16},{16,12},{20,24},{24,20},{28,0},{1,29},{... | collective-permute-start | bytes 49160 | tf_op jit(solution)/shard_map/ppermute | solution.py:796
  31.4 4.7 %collective-permute-start.7 = (f32[16,128]{1,0:T(8,128)S(1)}, f32[16,128]{1,0:T(8,128)S(1)}, u32[]{:S(2)}, u32[]{:S(2)}) collective-permute-start(f32[16,128]{1,0:T(8,128)S(1)} %get-tuple-element.58), channel_id=1, source_target_pairs={{0,3},{1,2},{2,1},{3,0},{4,7},{5,6},{6,5},{7,4},{8,11},{9,10},{10,... | collective-permute-start | bytes 24584 | tf_op jit(solution)/shard_map/ppermute | solution.py:796
  32.0 4.1 %collective-permute-start.8 = (f32[16,128]{1,0:T(8,128)S(1)}, f32[16,128]{1,0:T(8,128)S(1)}, u32[]{:S(2)}, u32[]{:S(2)}) collective-permute-start(f32[16,128]{1,0:T(8,128)S(1)} %get-tuple-element.59), channel_id=1, source_target_pairs={{0,2},{1,3},{2,0},{3,1},{4,6},{5,7},{6,4},{7,5},{8,10},{9,11},{10,... | collective-permute-start | bytes 24584 | tf_op jit(solution)/shard_map/ppermute | solution.py:796
  33.5 3.7 %collective-permute-start.9 = (f32[16,128]{1,0:T(8,128)S(1)}, f32[16,128]{1,0:T(8,128)S(1)}, u32[]{:S(2)}, u32[]{:S(2)}) collective-permute-start(f32[16,128]{1,0:T(8,128)S(1)} %get-tuple-element.60), channel_id=1, source_target_pairs={{0,1},{1,0},{2,3},{3,2},{4,5},{5,4},{6,7},{7,6},{8,9},{9,8},{10,11... | collective-permute-start | bytes 24584 | tf_op jit(solution)/shard_map/ppermute | solution.py:796
  37.1 10.4 %copy-start = (f32[512,128]{1,0:T(8,128)S(1)}, f32[512,128]{1,0:T(8,128)}, u32[]{:S(2)}) copy-start(f32[512,128]{1,0:T(8,128)} %solution_ref.1) | copy-start | bytes 786436
